TPU v7x, 512 devices: a whole 4x8x8 slice. The times are simulated.
512 devices in a mesh: inst: 32 (over z, x), tp: 16 (over y, core).
Axes of the slice: x: 4, y: 8, z: 8, core: 2. Of those that a mesh axis runs over, the one named last changes fastest.
Arguments:
- pool: bfloat16 [1280, 16, 2, 64, 128], P('inst', 'tp'), may hold values from -6 to 6
- sectioning: bfloat16 [1024, 16, 2, 64, 128], P('inst', 'tp'), may hold values from -6 to 6
- spill_to: int32 [1024], P('inst'), may hold values from 0 to 31, as said below
- tables: int32 [32, 111, 2], replicated, may hold values from -1 to 103, as said below
- lengths: int32 [32], replicated, may hold values from 4097 to 14208, as said below
- queries: bfloat16 [32, 4, 64, 128], P('inst', None, 'tp'), may hold values from -64 to 64
- new_kv: bfloat16 [32, 4, 2, 8, 128], P('inst'), may hold values from -6 to 6
Outputs:
- attended: bfloat16 [32, 4, 64, 128], P('inst', None, 'tp')
- lent: bfloat16 [2048, 16, 2, 64, 128], P('inst', 'tp')
Inputs may be any that keep to these rules, and one draw needn't show every extreme that they name: `spill_to`: the sectioned pages of one instance go at most 2 times to the same instance (possibly itself); on every instance some destination receives exactly 2 of them. tables[r, n] = (instance, slot) holding page n of request r, and (-1, -1) beyond the request's pages. Slots below 40 are resident; slot 40 + i * 2 + k is the k-th page that instance i lends there, counted in sectioning order. Every resident slot holds exactly one page of some request; request r is owned by instance r, and its last 32 pages are that instance's sectioned pages in sectioning order. Request r has ceil(lengths[r] / 128) pages, all listed in tables.
All inputs are finite; a program needn't handle non-finite values.
Results may differ from a plain program's by a relative error of at most 0.0035.
Values may be sent and summed in bfloat16 or wider, within the bound.
No kernel may reach another device: no remote copies, remote signals or barrier semaphores. Data moves between devices by JAX's collectives and lax.ppermute only.
A program may use at most 128 MiB of HBM per device.

v0:
```python
import jax
import jax.numpy as jnp
from jax import lax
from jax.sharding import PartitionSpec as P

QH = 64
KVH = 8
PAGE = 128
CAP = 2


NEG = -1e30


def partner_2(value, axis, distance):
    return lax.ppermute(value, axis, [(i, i ^ 1 << distance) for i in range(lax.axis_size(axis))])


def combine(first, second):
    out_first, sum_first, max_first = first
    out_second, sum_second, max_second = second
    joint_max = jnp.maximum(max_first, max_second)
    weight_first = jnp.exp(max_first - joint_max)
    weight_second = jnp.exp(max_second - joint_max)
    joined_out = out_first * weight_first[..., None] + out_second * weight_second[..., None]
    return (joined_out, sum_first * weight_first + sum_second * weight_second, joint_max)


def pick_heads(parts, first_head, head_count):
    return tuple((lax.dynamic_slice_in_dim(member, first_head, head_count, 2) for member in parts))


def shards(pool, sectioning, spill_to, tables, lengths, queries, new_kv):
    inst_count = lax.axis_size("inst")
    inst_index = lax.axis_index("inst")
    tp_index = lax.axis_index("tp")
    resident = pool.shape[0]
    sectioned_count = sectioning.shape[0]
    kv_local = pool.shape[1]
    half_len = pool.shape[3]
    head_dim = pool.shape[4]
    requests = tables.shape[0]
    max_pages = tables.shape[1]
    step_count = queries.shape[1]
    local_heads = queries.shape[2]
    owned = queries.shape[0]
    lent_slots = inst_count * CAP
    group_size = QH // KVH
    pair_side = tp_index % 2
    score_scale = head_dim ** (-0.5)
    section_order = jnp.arange(sectioned_count, dtype=jnp.int32)
    same_dest = spill_to[:, None] == spill_to[None, :]
    dest_rank = jnp.sum(
        jnp.where(same_dest & (section_order[None, :] < section_order[:, None]), 1, 0), axis=1
    )
    target = spill_to * CAP + dest_rank
    hit_table = target[None, :] == jnp.arange(lent_slots, dtype=jnp.int32)[:, None]
    source_row = jnp.sum(jnp.where(hit_table, section_order[None, :], 0), axis=1)
    filled = jnp.any(hit_table, axis=1)
    outgoing = jnp.where(
        filled[:, None, None, None, None], sectioning[source_row], jnp.zeros((), sectioning.dtype)
    )
    lent_pages = lax.all_to_all(outgoing, "inst", split_axis=0, concat_axis=0, tiled=True)
    holder = tables[:, :, 0]
    slot_index = tables[:, :, 1]
    total_slots = resident + lent_slots
    slot_ids = jnp.arange(total_slots, dtype=jnp.int32)
    matches = (holder == inst_index)[:, :, None] & (
        slot_index[:, :, None] == slot_ids[None, None, :]
    )
    onehot = jnp.any(matches, axis=1)
    page_number = jnp.arange(max_pages, dtype=jnp.int32)
    page_room = jnp.clip(lengths[:, None] - page_number[None, :] * PAGE, 0, PAGE)
    valid_tokens = jnp.sum(jnp.where(matches, page_room[:, :, None], 0), axis=(0, 1))
    owner_of = jnp.sum(jnp.where(onehot, jnp.arange(requests, dtype=jnp.int32)[:, None], 0), axis=0)
    partner = partner_2(queries, "tp", 0)
    group_queries = jnp.where(
        pair_side == 0,
        jnp.concatenate([queries, partner], 2),
        jnp.concatenate([partner, queries], 2),
    )
    everyone = lax.all_gather(group_queries, "inst", axis=0, tiled=True)
    heads_here = everyone.shape[2]
    stored = jnp.concatenate([pool, lent_pages], axis=0)
    key_rows = stored[:, :, 0]
    value_rows = stored[:, :, 1]
    token_pos = pair_side * half_len + jnp.arange(half_len, dtype=jnp.int32)
    page_mask = token_pos[None, :] < valid_tokens[:, None]
    chosen = everyone[owner_of].reshape(total_slots, step_count, kv_local, group_size, head_dim)
    scores = (
        jnp.einsum("askgd,aktd->aksgt", chosen, key_rows, preferred_element_type=jnp.float32)
        * score_scale
    )
    full_mask = page_mask[:, None, None, None, :]
    masked = jnp.where(full_mask, scores, NEG)
    slot_max = jnp.max(masked, axis=4)
    request_max = jnp.max(jnp.where(onehot[:, :, None, None, None], slot_max[None], NEG), axis=1)
    slot_ref = request_max[owner_of]
    weights = jnp.where(full_mask, jnp.exp(masked - slot_max[..., None]), 0.0)
    slot_sum = jnp.sum(weights, axis=4)
    slot_out = jnp.einsum(
        "aksgt,aktd->aksgd",
        weights.astype(jnp.bfloat16),
        value_rows,
        preferred_element_type=jnp.float32,
    )
    rescale = jnp.exp(slot_max - slot_ref)
    slot_out = slot_out * rescale[..., None]
    slot_sum = slot_sum * rescale
    indicator = onehot.astype(jnp.float32)
    part_out = jnp.einsum("ra,aksgd->rskgd", indicator, slot_out, precision=lax.Precision.HIGHEST)
    part_sum = jnp.einsum("ra,aksg->rskg", indicator, slot_sum, precision=lax.Precision.HIGHEST)
    part_max = jnp.transpose(request_max, (0, 2, 1, 3))
    parts = (
        part_out.reshape(requests, step_count, heads_here, head_dim),
        part_sum.reshape(requests, step_count, heads_here),
        part_max.reshape(requests, step_count, heads_here),
    )
    shaped = [
        member.reshape((inst_count, member.shape[0] // inst_count) + member.shape[1:])
        for member in parts
    ]
    arrived = (
        lax.all_to_all(shaped[0], "inst", split_axis=0, concat_axis=0, tiled=True),
        lax.all_to_all(shaped[1], "inst", split_axis=0, concat_axis=0, tiled=True),
        lax.all_to_all(shaped[2], "inst", split_axis=0, concat_axis=0, tiled=True),
    )
    joint_max = jnp.max(arrived[2], axis=0)
    scaling = jnp.exp(arrived[2] - joint_max[None])
    parts = (
        jnp.sum(arrived[0] * scaling[..., None], axis=0),
        jnp.sum(arrived[1] * scaling, axis=0),
        joint_max,
    )
    keep_part = pick_heads(parts, pair_side * local_heads, local_heads)
    give_part = pick_heads(parts, (1 - pair_side) * local_heads, local_heads)
    other_half = partner_2((give_part[0], give_part[1], give_part[2]), "tp", 0)
    parts = combine(keep_part, other_half)
    kv_own = max(1, local_heads // group_size)
    kv_start = tp_index * local_heads // group_size
    fresh_keys = lax.dynamic_slice_in_dim(new_kv[:, :, 0], kv_start, kv_own, 2)
    fresh_values = lax.dynamic_slice_in_dim(new_kv[:, :, 1], kv_start, kv_own, 2)
    heads_per_kv = local_heads // kv_own
    own_queries = queries.reshape(owned, step_count, kv_own, heads_per_kv, head_dim)
    new_scores = (
        jnp.einsum("rskgd,rjkd->rskgj", own_queries, fresh_keys, preferred_element_type=jnp.float32)
        * score_scale
    )
    step_order = jnp.arange(step_count, dtype=jnp.int32)
    causal = (step_order[None, :] <= step_order[:, None])[None, :, None, None, :]
    new_scores = jnp.where(causal, new_scores, NEG)
    new_max = jnp.max(new_scores, axis=4)
    old_out = parts[0].reshape(owned, step_count, kv_own, heads_per_kv, head_dim)
    old_sum = parts[1].reshape(owned, step_count, kv_own, heads_per_kv)
    old_max = parts[2].reshape(owned, step_count, kv_own, heads_per_kv)
    joint_max = jnp.maximum(old_max, new_max)
    old_weight = jnp.exp(old_max - joint_max)
    new_factor = jnp.exp(new_max - joint_max)
    new_weights = jnp.where(causal, jnp.exp(new_scores - new_max[..., None]), 0.0)
    weight_sum = old_sum * old_weight + jnp.sum(new_weights, axis=4) * new_factor
    new_mix = jnp.einsum(
        "rskgj,rjkd->rskgd",
        new_weights.astype(jnp.bfloat16),
        fresh_values,
        preferred_element_type=jnp.float32,
    )
    mixture = old_out * old_weight[..., None] + new_mix * new_factor[..., None]
    attended = (
        (mixture / weight_sum[..., None])
        .reshape(owned, step_count, local_heads, head_dim)
        .astype(jnp.bfloat16)
    )
    return (attended, lent_pages)


def solution(mesh):
    placed = (
        P("inst", "tp", None, None, None),
        P("inst", "tp", None, None, None),
        P("inst"),
        P(),
        P(),
        P("inst", None, "tp", None),
        P("inst", None, None, None, None),
    )
    return jax.shard_map(
        shards,
        mesh=mesh,
        in_specs=placed,
        out_specs=(P("inst", None, "tp", None), P("inst", "tp", None, None, None)),
        check_vma=False,
    )
```

profile of v0, /device:TPU:56, one launch (start us, length us, event | category | flops | bytes accessed | tf_op | source)
XLA Modules:
  0.0 178.1 jit_solution(1346812984937425800)
XLA Ops:
  0.6 0.9 select_reduce_fusion.3
  1.6 0.7 multiply_add_fusion
  2.2 0.1 select_reduce_fusion.2
  2.3 0.1 fusion.21
  2.5 1.0 gather_fusion.1
  3.4 1.5 fusion
  5.0 13.3 %all-to-all-start = ((bf16[64,1,2,64,128]{4,3,2,1,0:T(8,128)(2,1)}), bf16[64,1,2,64,128]{4,3,2,1,0:T(8,128)(2,1)S(1)}, u32[]{:S(2)}, u32[]{:S(2)}) async-start(bf16[64,1,2,64,128]{4,3,2,1,0:T(8,128)(2,1)} %fusion), calls=%async_computation | async-start | bytes 4194304 | tf_op jit(solution)/shard_map/all_to_all | solution.py:63
  18.3 1.9 %collective-permute-start = (bf16[1,4,4,128]{3,2,1,0:T(4,128)(2,1)S(1)}, bf16[1,4,4,128]{3,2,1,0:T(4,128)(2,1)S(1)}, u32[]{:S(2)}, u32[]{:S(2)}) collective-permute-start(bf16[1,4,4,128]{3,2,1,0:T(4,128)(2,1)S(1)} %copy-done.6), channel_id=1, source_target_pairs={{0,1},{1,0},{2,3},{3,2},{4,5},{5,4},{6,7},{7,6},{8,9},{9,8},{10,11... | collective-permute-start | bytes 12296 | tf_op jit(solution)/shard_map/ppermute | solution.py:16
  20.4 0.6 fusion.6
  21.0 0.1 convolution_multiply_fusion
  21.2 0.1 fusion.28
  21.3 2.6 %constant_dynamic-update-slice_fusion.1 = bf16[104,1,2,64,128]{4,3,2,1,0:T(8,128)(2,1)} fusion(bf16[40,1,2,64,128]{4,3,2,1,0:T(8,128)(2,1)} %param.7), kind=kLoop, calls=%fused_computation.61 | loop fusion | bytes 2621440
  23.8 0.1 subtract_clamp_fusion
  23.9 0.7 select_reduce_fusion
  24.6 0.1 broadcast_compare_fusion
  24.7 83.0 %all_gather.3 = bf16[32,4,8,128]{3,2,1,0:T(8,128)(2,1)S(1)} all-gather(bf16[1,4,8,128]{3,2,1,0:T(8,128)(2,1)S(1)} %maximum_select_fusion), channel_id=1, replica_groups=mesh['inst'=32,'tp'=16] {'inst'}, dimensions={0}, use_global_device_ids=true | all-gather | bytes 270336 | tf_op jit(solution)/shard_map/all_gather | solution.py:82
  107.7 1.6 gather_fusion
  109.3 1.6 constant_dynamic-update-slice_fusion
  110.9 3.7 %fusion.57 = (f32[104,4,8]{2,1,0:T(4,128)S(1)}, f32[104,4,8,64]{3,2,1,0:T(8,128)}) fusion(bf16[104,4,8,128]{3,2,1,0:T(8,128)(2,1)S(1)} %copy-done.2, bf16[104,1,2,64,128]{4,3,2,1,0:T(8,128)(2,1)} %constant_dynamic-update-slice_fusion, pred[104,64]{1,0:T(8,128)(4,1)S(1)} %broadcast_compare_fusion), kind=kOutput, calls=%fused_computation.102 | convolution fusion | flops 55161600 | bytes 3427840 | tf_op jit(solution)/shard_map/askgd,aktd->aksgt/dot_general | solution.py:91
  114.6 0.1 copy.39
  114.7 0.9 select_reduce_fusion.1
  115.6 2.2 %gather_fusion.2 = f32[104,4,8]{2,1,0:T(4,128)} fusion(f32[32,4,8]{2,1,0:T(4,128)} %select_reduce_fusion.1, s32[1024]{0:T(1024)S(1)} %pad_clamp_fusion.1), kind=kCustom, calls=%fused_computation.2 | custom fusion | bytes 27040 | tf_op jit(solution)/shard_map/gather | solution.py:98
  117.9 7.6 %all-to-all-start.2 = ((f32[32,1,4,8]{3,2,1,0:T(4,128)}), f32[32,1,4,8]{3,2,1,0:T(4,128)S(1)}, u32[]{:S(2)}, u32[]{:S(2)}) async-start(f32[32,1,4,8]{3,2,1,0:T(4,128)} %bitcast.21), calls=%async_computation.2 | async-start | bytes 131072 | tf_op jit(solution)/shard_map/all_to_all | solution.py:126
  125.5 2.6 %fusion.8 = f32[104,4,8]{2,1,0:T(4,128)S(1)} fusion(f32[104,4,8,64]{3,2,1,0:T(8,128)} %get-tuple-element.22, f32[104,4,8]{2,1,0:T(4,128)S(1)} %get-tuple-element.21, pred[104,64]{1,0:T(8,128)(4,1)S(1)} %broadcast_compare_fusion), kind=kLoop, calls=%fused_computation.18 | loop fusion | flops 635648 | bytes 885248 | tf_op jit(solution)/shard_map/reduce_sum | solution.py:100
  128.2 3.7 %fusion.7 = f32[104,4,8,128]{3,2,1,0:T(8,128)} fusion(bf16[104,1,2,64,128]{4,3,2,1,0:T(8,128)(2,1)} %constant_dynamic-update-slice_fusion, f32[104,4,8,64]{3,2,1,0:T(8,128)S(1)} %copy-done.1, f32[104,4,8]{2,1,0:T(4,128)S(1)} %bitcast.174, f32[104,4,8]{2,1,0:T(4,128)S(1)} %get-tuple-element.21, pred[104,64]{1,0:T(8,128)(4,1)S(1)} %broadcast_compare_fusion), kind=kOutput, calls=%fused_computation.17 | convolution fusion | flops 55590912 | bytes 4293120 | tf_op jit(solution)/shard_map/aksgt,aktd->aksgd/dot_general | solution.py:101
  131.9 0.3 convolution_bitcast_fusion
  132.2 0.7 copy.46
  132.9 2.5 %all-to-all-done.2 = f32[32,1,4,8]{3,2,1,0:T(4,128)S(1)} async-done(((f32[32,1,4,8]{3,2,1,0:T(4,128)}), f32[32,1,4,8]{3,2,1,0:T(4,128)S(1)}, u32[]{:S(2)}, u32[]{:S(2)}) %all-to-all-start.2) | async-done | bytes 4128 | tf_op jit(solution)/shard_map/all_to_all | solution.py:126
  135.4 7.2 %all-to-all-start.3 = ((f32[32,1,4,8]{3,2,1,0:T(4,128)}), f32[32,1,4,8]{3,2,1,0:T(4,128)S(1)}, u32[]{:S(2)}, u32[]{:S(2)}) async-start(f32[32,1,4,8]{3,2,1,0:T(4,128)} %copy.46), calls=%async_computation.3 | async-start | bytes 131072 | tf_op jit(solution)/shard_map/all_to_all | solution.py:125
  142.7 3.0 %fusion.10 = f32[32,1,4,8,128]{4,0,3,2,1:T(8,128)S(1)} fusion(f32[104,4,8,128]{3,2,1,0:T(8,128)} %fusion.7, pred[32,104]{1,0:T(8,128)(4,1)S(1)} %fusion.6), kind=kOutput, calls=%fused_computation.20 | convolution fusion | flops 163577856 | bytes 2231552 | tf_op jit(solution)/shard_map/ra,aksgd->rskgd/dot_general | solution.py:111
  145.7 1.1 copy.41
  146.8 6.2 %all-to-all-done.3 = f32[32,1,4,8]{3,2,1,0:T(4,128)S(1)} async-done(((f32[32,1,4,8]{3,2,1,0:T(4,128)}), f32[32,1,4,8]{3,2,1,0:T(4,128)S(1)}, u32[]{:S(2)}, u32[]{:S(2)}) %all-to-all-start.3) | async-done | bytes 4128 | tf_op jit(solution)/shard_map/all_to_all | solution.py:125
  153.0 4.6 %all-to-all-start.1 = ((f32[32,1,4,8,128]{4,3,2,1,0:T(8,128)}), f32[32,1,4,8,128]{4,3,2,1,0:T(8,128)}, u32[]{:S(2)}, u32[]{:S(2)}) async-start(f32[32,1,4,8,128]{4,3,2,1,0:T(8,128)} %copy.41), calls=%async_computation.1 | async-start | bytes 1048576 | tf_op jit(solution)/shard_map/all_to_all | solution.py:124
  157.7 0.1 fusion.33
  157.8 0.1 copy.44
  157.9 0.1 dynamic-slice_bitcast_fusion.2
  158.0 1.9 %collective-permute-start.1 = (f32[1,4,4]{2,1,0:T(4,128)S(1)}, f32[1,4,4]{2,1,0:T(4,128)S(1)}, u32[]{:S(2)}, u32[]{:S(2)}) collective-permute-start(f32[1,4,4]{2,1,0:T(4,128)S(1)} %dynamic-slice_bitcast_fusion.2), channel_id=1, source_target_pairs={{0,1},{1,0},{2,3},{3,2},{4,5},{5,4},{6,7},{7,6},{8,9},{9,8},{10,11... | collective-permute-start | bytes 200 | tf_op jit(solution)/shard_map/ppermute | solution.py:16
  160.0 0.1 dynamic-slice_bitcast_fusion.1
  160.1 2.4 %collective-permute-start.3 = (f32[1,4,4]{2,1,0:T(4,128)S(1)}, f32[1,4,4]{2,1,0:T(4,128)S(1)}, u32[]{:S(2)}, u32[]{:S(2)}) collective-permute-start(f32[1,4,4]{2,1,0:T(4,128)S(1)} %dynamic-slice_bitcast_fusion.1), channel_id=1, source_target_pairs={{0,1},{1,0},{2,3},{3,2},{4,5},{5,4},{6,7},{7,6},{8,9},{9,8},{10,11... | collective-permute-start | bytes 200 | tf_op jit(solution)/shard_map/ppermute | solution.py:16
  162.5 0.1 fusion.50
  162.5 0.7 collective-permute-done.3
  163.3 0.1 fusion.36
  163.3 8.4 %all-to-all-done.1 = f32[32,1,4,8,128]{4,3,2,1,0:T(8,128)} async-done(((f32[32,1,4,8,128]{4,3,2,1,0:T(8,128)}), f32[32,1,4,8,128]{4,3,2,1,0:T(8,128)}, u32[]{:S(2)}, u32[]{:S(2)}) %all-to-all-start.1) | async-done | bytes 524320 | tf_op jit(solution)/shard_map/all_to_all | solution.py:124
  171.7 1.2 multiply_reduce_fusion
  173.0 1.9 %collective-permute-start.2 = (f32[1,4,4,128]{3,2,1,0:T(4,128)S(1)}, f32[1,4,4,128]{3,2,1,0:T(4,128)S(1)}, u32[]{:S(2)}, u32[]{:S(2)}) collective-permute-start(f32[1,4,4,128]{3,2,1,0:T(4,128)S(1)} %dynamic-slice_bitcast_fusion), channel_id=1, source_target_pairs={{0,1},{1,0},{2,3},{3,2},{4,5},{5,4},{6,7},{7,6},{8,9},{9,8},{10,11... | collective-permute-start | bytes 24584 | tf_op jit(solution)/shard_map/ppermute | solution.py:16
  174.9 1.1 collective-permute-done.2
  176.1 0.7 fusion.31
  176.8 1.3 copy.81
  (38 shorter events, 0.4 us)
Async XLA Ops:
  0.6 1.8 %copy-start = (bf16[32,1,2,64,128]{4,3,2,1,0:T(8,128)(2,1)S(1)}, bf16[32,1,2,64,128]{4,3,2,1,0:T(8,128)(2,1)}, u32[]{:S(2)}) copy-start(bf16[32,1,2,64,128]{4,3,2,1,0:T(8,128)(2,1)} %param.8) | copy-start | bytes 3145732
  5.0 13.3 %copy-start.6 = (bf16[1,4,4,128]{3,2,1,0:T(4,128)(2,1)S(1)}, bf16[1,4,4,128]{3,2,1,0:T(4,128)(2,1)}, u32[]{:S(2)}) copy-start(bf16[1,4,4,128]{3,2,1,0:T(4,128)(2,1)} %param.12) | copy-start | bytes 12292
  5.0 15.3 %copy-start.5 = (bf16[1,4,2,8,128]{4,3,2,1,0:T(8,128)(2,1)S(1)}, bf16[1,4,2,8,128]{4,3,2,1,0:T(8,128)(2,1)}, u32[]{:S(2)}) copy-start(bf16[1,4,2,8,128]{4,3,2,1,0:T(8,128)(2,1)} %param.13) | copy-start | bytes 49156
  5.0 15.4 %copy-start.4 = (s32[32,111,2]{1,2,0:T(2,128)S(1)}, s32[32,111,2]{1,2,0:T(2,128)}, u32[]{:S(2)}) copy-start(s32[32,111,2]{1,2,0:T(2,128)} %param.10) | copy-start | bytes 85252
  5.0 104.3 %all-to-all-start = ((bf16[64,1,2,64,128]{4,3,2,1,0:T(8,128)(2,1)}), bf16[64,1,2,64,128]{4,3,2,1,0:T(8,128)(2,1)S(1)}, u32[]{:S(2)}, u32[]{:S(2)}) async-start(bf16[64,1,2,64,128]{4,3,2,1,0:T(8,128)(2,1)} %fusion), calls=%async_computation | async-start | bytes 4194304 | tf_op jit(solution)/shard_map/all_to_all | solution.py:63
  18.3 5.6 %copy-start.7 = (s32[32]{0:T(128)S(1)}, s32[32]{0:T(128)}, u32[]{:S(2)}) copy-start(s32[32]{0:T(128)} %param.11) | copy-start | bytes 388
  18.3 6.4 %collective-permute-start = (bf16[1,4,4,128]{3,2,1,0:T(4,128)(2,1)S(1)}, bf16[1,4,4,128]{3,2,1,0:T(4,128)(2,1)S(1)}, u32[]{:S(2)}, u32[]{:S(2)}) collective-permute-start(bf16[1,4,4,128]{3,2,1,0:T(4,128)(2,1)S(1)} %copy-done.6), channel_id=1, source_target_pairs={{0,1},{1,0},{2,3},{3,2},{4,5},{5,4},{6,7},{7,6},{8,9},{9,8},{10,11... | collective-permute-start | bytes 12296 | tf_op jit(solution)/shard_map/ppermute | solution.py:16
  109.3 1.6 copy-start.2
  117.9 17.6 %all-to-all-start.2 = ((f32[32,1,4,8]{3,2,1,0:T(4,128)}), f32[32,1,4,8]{3,2,1,0:T(4,128)S(1)}, u32[]{:S(2)}, u32[]{:S(2)}) async-start(f32[32,1,4,8]{3,2,1,0:T(4,128)} %bitcast.21), calls=%async_computation.2 | async-start | bytes 131072 | tf_op jit(solution)/shard_map/all_to_all | solution.py:126
  125.5 2.6 %copy-start.3 = (f32[104,4,8]{2,1,0:T(4,128)S(1)}, f32[104,4,8]{2,1,0:T(4,128)}, u32[]{:S(2)}) copy-start(f32[104,4,8]{2,1,0:T(4,128)} %gather_fusion.2) | copy-start | bytes 39940
  125.5 2.7 %copy-start.1 = (f32[104,4,8,64]{3,2,1,0:T(8,128)S(1)}, f32[104,4,8,64]{3,2,1,0:T(8,128)}, u32[]{:S(2)}) copy-start(f32[104,4,8,64]{3,2,1,0:T(8,128)} %get-tuple-element.22) | copy-start | bytes 2555908
  135.4 17.6 %all-to-all-start.3 = ((f32[32,1,4,8]{3,2,1,0:T(4,128)}), f32[32,1,4,8]{3,2,1,0:T(4,128)S(1)}, u32[]{:S(2)}, u32[]{:S(2)}) async-start(f32[32,1,4,8]{3,2,1,0:T(4,128)} %copy.46), calls=%async_computation.3 | async-start | bytes 131072 | tf_op jit(solution)/shard_map/all_to_all | solution.py:125
  153.0 18.7 %all-to-all-start.1 = ((f32[32,1,4,8,128]{4,3,2,1,0:T(8,128)}), f32[32,1,4,8,128]{4,3,2,1,0:T(8,128)}, u32[]{:S(2)}, u32[]{:S(2)}) async-start(f32[32,1,4,8,128]{4,3,2,1,0:T(8,128)} %copy.41), calls=%async_computation.1 | async-start | bytes 1048576 | tf_op jit(solution)/shard_map/all_to_all | solution.py:124
  158.0 4.5 %collective-permute-start.1 = (f32[1,4,4]{2,1,0:T(4,128)S(1)}, f32[1,4,4]{2,1,0:T(4,128)S(1)}, u32[]{:S(2)}, u32[]{:S(2)}) collective-permute-start(f32[1,4,4]{2,1,0:T(4,128)S(1)} %dynamic-slice_bitcast_fusion.2), channel_id=1, source_target_pairs={{0,1},{1,0},{2,3},{3,2},{4,5},{5,4},{6,7},{7,6},{8,9},{9,8},{10,11... | collective-permute-start | bytes 200 | tf_op jit(solution)/shard_map/ppermute | solution.py:16
  160.1 3.2 %collective-permute-start.3 = (f32[1,4,4]{2,1,0:T(4,128)S(1)}, f32[1,4,4]{2,1,0:T(4,128)S(1)}, u32[]{:S(2)}, u32[]{:S(2)}) collective-permute-start(f32[1,4,4]{2,1,0:T(4,128)S(1)} %dynamic-slice_bitcast_fusion.1), channel_id=1, source_target_pairs={{0,1},{1,0},{2,3},{3,2},{4,5},{5,4},{6,7},{7,6},{8,9},{9,8},{10,11... | collective-permute-start | bytes 200 | tf_op jit(solution)/shard_map/ppermute | solution.py:16
  173.0 3.1 %collective-permute-start.2 = (f32[1,4,4,128]{3,2,1,0:T(4,128)S(1)}, f32[1,4,4,128]{3,2,1,0:T(4,128)S(1)}, u32[]{:S(2)}, u32[]{:S(2)}) collective-permute-start(f32[1,4,4,128]{3,2,1,0:T(4,128)S(1)} %dynamic-slice_bitcast_fusion), channel_id=1, source_target_pairs={{0,1},{1,0},{2,3},{3,2},{4,5},{5,4},{6,7},{7,6},{8,9},{9,8},{10,11... | collective-permute-start | bytes 24584 | tf_op jit(solution)/shard_map/ppermute | solution.py:16
where the time goes:
time: 180 us; the launch traced here: 178 us
  blocking collectives  83 us (46%)
  starting transfers between devices  40.9 us (23%)
  waiting for transfers between devices  19 us (11%)
  local copies, waits for them, and re-layouts  12.6 us (7%)
  matrix products  11.6 us (6%)
  other arithmetic  10.1 us (6%)
    all_gather x1, blocking collectives, shards(): everyone = lax.all_gather(group_queries, 'inst', axis=0, tiled=True)  83 us
    all_to_all x1, starting transfers between devices, shards(): lax.all_to_all(outgoing, 'inst', split_axis=0, concat_axis=0, tiled=True)  13.3 us
    all_to_all x1, waiting for transfers between devices, shards(): lax.all_to_all(shaped[0], 'inst', split_axis=0, concat_axis=0, tiled=True)  8.39 us
    ppermute x4, starting transfers between devices, partner_2(): lax.ppermute(value, axis, [(i, i ^ 1 << distance) for i in range(lax.axis...  8.15 us
    all_to_all x1, starting transfers between devices, shards(): lax.all_to_all(shaped[2], 'inst', split_axis=0, concat_axis=0, tiled=True)  7.6 us
    all_to_all x1, starting transfers between devices, shards(): lax.all_to_all(shaped[1], 'inst', split_axis=0, concat_axis=0, tiled=True)  7.24 us
    all_to_all x1, waiting for transfers between devices, shards(): lax.all_to_all(shaped[1], 'inst', split_axis=0, concat_axis=0, tiled=True)  6.19 us
    all_to_all x1, starting transfers between devices, shards(): lax.all_to_all(shaped[0], 'inst', split_axis=0, concat_axis=0, tiled=True)  4.62 us
  transfers between devices with their start and end apart: 8, of which 5 were waited for; matrix products, arithmetic and copies ran while one was open for 10% of the time, Pallas kernels for 0%

commit v1 on v0

v1 whole, which is shorter than its diff:
```python
import functools

import jax
import jax.numpy as jnp
from jax import lax
from jax.experimental import pallas as pl
from jax.experimental.pallas import tpu as pltpu
from jax.sharding import Mesh, PartitionSpec as P

PAGE = 128
CAP = 2
NEG = -1e30
NT = (((1,), (1,)), ((), ()))


def pack_kernel(spill_ref, section_ref, query_ref, out_ref, zeros, spread, count, page_sems, query_sem):
    insts = out_ref.shape[0]
    sectioned, rows = section_ref.shape[0], section_ref.shape[1]
    spread[...] = jnp.broadcast_to(query_ref[...][None], spread.shape)
    query_copy = pltpu.make_async_copy(
        spread, out_ref.at[:, pl.ds(CAP * rows, query_ref.shape[0])], query_sem
    )
    query_copy.start()
    zeros[...] = jnp.zeros_like(zeros)

    def slot_copy(source, dest, rank):
        start = pl.multiple_of(rank * rows, rows)
        return pltpu.make_async_copy(
            source, out_ref.at[dest, pl.ds(start, rows)], page_sems.at[dest * CAP + rank]
        )

    for dest in range(insts):
        count[dest] = 0

    @pl.loop(0, sectioned)
    def _(row):
        dest = spill_ref[row]
        rank = count[dest]
        count[dest] = rank + 1
        slot_copy(section_ref.at[row], dest, rank).start()

    @pl.loop(0, insts)
    def _(dest):
        filled = count[dest]
        for rank in range(CAP):

            @pl.when(filled <= rank)
            def _():
                slot_copy(zeros, dest, rank).start()

    @pl.loop(0, insts)
    def _(dest):
        for rank in range(CAP):
            slot_copy(zeros, dest, rank).wait()

    query_copy.wait()


def pack(spill_to, section_pages, query_rows, insts):
    rows, head_dim = section_pages.shape[1:]
    query_count = query_rows.shape[0]
    return pl.pallas_call(
        pack_kernel,
        out_shape=jax.ShapeDtypeStruct((insts, CAP * rows + query_count, head_dim), section_pages.dtype),
        in_specs=[
            pl.BlockSpec(memory_space=pltpu.SMEM),
            pl.BlockSpec(memory_space=pl.ANY),
            pl.BlockSpec(memory_space=pltpu.VMEM),
        ],
        out_specs=pl.BlockSpec(memory_space=pl.ANY),
        scratch_shapes=[
            pltpu.VMEM((rows, head_dim), section_pages.dtype),
            pltpu.VMEM((insts, query_count, head_dim), query_rows.dtype),
            pltpu.SMEM((insts,), jnp.int32),
            pltpu.SemaphoreType.DMA((insts * CAP,)),
            pltpu.SemaphoreType.DMA,
        ],
        name="pack",
    )(spill_to, section_pages, query_rows)


def resident_kernel(score_scale, owner_ref, arrived_ref, kv_ref, out_ref, asked, score, top, total, mix, sem):
    requests, query_count = asked.shape[0], asked.shape[1]
    slots = kv_ref.shape[1]
    query_copy = pltpu.make_async_copy(
        arrived_ref.at[:, pl.ds(arrived_ref.shape[1] - query_count, query_count)], asked, sem
    )
    query_copy.start()
    top[...] = jnp.full(top.shape, NEG, jnp.float32)
    total[...] = jnp.zeros_like(total)
    mix[...] = jnp.zeros_like(mix)
    query_copy.wait()
    for slot in range(slots):
        owner = owner_ref[slot]
        keys = jnp.concatenate([kv_ref[0, slot, 0], kv_ref[1, slot, 0]], axis=0)
        found = lax.dot_general(asked[owner], keys, NT, preferred_element_type=jnp.float32) * score_scale
        score[slot] = found
        top[owner] = jnp.maximum(top[owner], found)
    for request in range(requests):
        top[request] = jnp.broadcast_to(jnp.max(top[request], axis=1, keepdims=True), top.shape[1:])
    for slot in range(slots):
        owner = owner_ref[slot]
        weights = jnp.exp(score[slot] - top[owner])
        values = jnp.concatenate([kv_ref[0, slot, 1], kv_ref[1, slot, 1]], axis=0)
        total[owner] = total[owner] + weights
        mix[owner] = mix[owner] + jnp.dot(
            weights.astype(jnp.bfloat16), values, preferred_element_type=jnp.float32
        )
    lane = lax.broadcasted_iota(jnp.int32, top.shape[1:], 1)
    for request in range(requests):
        norm = jnp.sum(total[request], axis=1, keepdims=True)
        held = norm > 0.0
        safe = jnp.where(held, norm, 1.0)
        out_ref[request, 0:query_count] = (mix[request] / safe).astype(jnp.bfloat16)
        level = jnp.where(held, top[request] + jnp.log(safe), NEG)
        high = level.astype(jnp.bfloat16).astype(jnp.float32)
        middle = (level - high).astype(jnp.bfloat16).astype(jnp.float32)
        low = level - high - middle
        terms = jnp.where(lane == 0, high, jnp.where(lane == 1, middle, jnp.where(lane == 2, low, 0.0)))
        out_ref[request, query_count : 2 * query_count] = terms.astype(jnp.bfloat16)


def resident(owner_of, arrived, pool_both, score_scale, query_count):
    requests, head_dim = arrived.shape[0], arrived.shape[2]
    slots = pool_both.shape[1]
    tokens = 2 * pool_both.shape[3]
    per_request = pltpu.VMEM((requests, query_count, head_dim), jnp.float32)
    return pl.pallas_call(
        functools.partial(resident_kernel, score_scale),
        out_shape=jax.ShapeDtypeStruct((requests, 2 * query_count, head_dim), jnp.bfloat16),
        in_specs=[
            pl.BlockSpec(memory_space=pltpu.SMEM),
            pl.BlockSpec(memory_space=pl.ANY),
            pl.BlockSpec(memory_space=pltpu.VMEM),
        ],
        out_specs=pl.BlockSpec(memory_space=pltpu.VMEM),
        scratch_shapes=[
            pltpu.VMEM((requests, query_count, head_dim), jnp.bfloat16),
            pltpu.VMEM((slots, query_count, tokens), jnp.float32),
            pltpu.VMEM((requests, query_count, tokens), jnp.float32),
            pltpu.VMEM((requests, query_count, tokens), jnp.float32),
            per_request,
            pltpu.SemaphoreType.DMA,
        ],
        compiler_params=pltpu.CompilerParams(vmem_limit_bytes=24 * 1024 * 1024),
        name="resident",
    )(owner_of, arrived, pool_both)


def finish_kernel(parts_ref, mix_ref, total_ref, top_ref, out_ref):
    query_count = mix_ref.shape[0]
    parts = parts_ref[...].astype(jnp.float32)
    outs, levels = parts[:, :query_count], parts[:, query_count:]
    levels = jnp.sum(levels, axis=2, keepdims=True)
    own_top = top_ref[...]
    joint = jnp.maximum(jnp.max(levels, axis=0), own_top)
    factor = jnp.exp(levels - joint[None])
    own_factor = jnp.exp(own_top - joint)
    norm = jnp.sum(factor, axis=0) + total_ref[...] * own_factor
    mixture = jnp.sum(outs * factor, axis=0) + mix_ref[...] * own_factor
    out_ref[...] = (mixture / norm).astype(jnp.bfloat16)


def finish(parts, own_mix, own_total, own_top):
    return pl.pallas_call(
        finish_kernel,
        out_shape=jax.ShapeDtypeStruct(own_mix.shape, jnp.bfloat16),
        in_specs=[pl.BlockSpec(memory_space=pltpu.VMEM)] * 4,
        out_specs=pl.BlockSpec(memory_space=pltpu.VMEM),
        name="finish",
    )(parts, own_mix, own_total, own_top)


def own_partial(query_rows, section_both, new_kv, length, pair_index, heads, score_scale):
    sectioned, half_len = section_both.shape[1], section_both.shape[3]
    steps = new_kv.shape[1]
    key_rows, value_rows = section_both[:, :, 0], section_both[:, :, 1]
    cached = (
        jnp.einsum("qd,bntd->qbnt", query_rows, key_rows, preferred_element_type=jnp.float32) * score_scale
    )
    page_count = (length + PAGE - 1) // PAGE
    page = page_count - sectioned + jnp.arange(sectioned, dtype=jnp.int32)
    position = (
        page[None, :, None] * PAGE
        + jnp.arange(2, dtype=jnp.int32)[:, None, None] * half_len
        + jnp.arange(half_len, dtype=jnp.int32)[None, None, :]
    )
    cached_mask = (position < length)[None]
    fresh = lax.dynamic_slice_in_dim(new_kv[0], pair_index, 1, 2)[:, :, 0]
    recent = (
        jnp.einsum("qd,jd->qj", query_rows, fresh[:, 0], preferred_element_type=jnp.float32) * score_scale
    )
    step = jnp.arange(query_rows.shape[0], dtype=jnp.int32) // heads
    recent_mask = jnp.arange(steps, dtype=jnp.int32)[None, :] <= step[:, None]
    cached = jnp.where(cached_mask, cached, NEG)
    recent = jnp.where(recent_mask, recent, NEG)
    top = jnp.maximum(jnp.max(cached, axis=(1, 2, 3)), jnp.max(recent, axis=1))[:, None]
    cached_weights = jnp.where(cached_mask, jnp.exp(cached - top[:, :, None, None]), 0.0)
    recent_weights = jnp.where(recent_mask, jnp.exp(recent - top), 0.0)
    total = jnp.sum(cached_weights, axis=(1, 2, 3)) + jnp.sum(recent_weights, axis=1)
    mix = jnp.einsum(
        "qbnt,bntd->qd", cached_weights.astype(jnp.bfloat16), value_rows, preferred_element_type=jnp.float32
    ) + jnp.einsum("qj,jd->qd", recent_weights.astype(jnp.bfloat16), fresh[:, 1], preferred_element_type=jnp.float32)
    return mix, jnp.broadcast_to(total[:, None], mix.shape), jnp.broadcast_to(top, mix.shape)


def shards(pool, sectioning, spill_to, tables, lengths, queries, new_kv):
    insts = lax.axis_size("inst")
    inst_index = lax.axis_index("inst")
    pair_index = lax.axis_index("pair")
    resident_slots, half_len, head_dim = pool.shape[0], pool.shape[3], pool.shape[4]
    sectioned = sectioning.shape[0]
    heads = queries.shape[2]
    query_count = queries.shape[1] * heads
    score_scale = head_dim ** (-0.5)
    query_rows = queries.reshape(query_count, head_dim)
    section_pages = sectioning.reshape(sectioned, 2 * half_len, head_dim)

    outgoing = pack(spill_to, section_pages, query_rows, insts)
    arrived = lax.all_to_all(outgoing, "inst", split_axis=0, concat_axis=0, tiled=True)

    pool_both = lax.all_gather(pool.reshape(pool.shape[0], 2, half_len, head_dim), "core", axis=0)
    section_both = lax.all_gather(sectioning.reshape(sectioned, 2, half_len, head_dim), "core", axis=0)
    held_here = (tables[:, :, 0] == inst_index)[:, :, None] & (
        tables[:, :, 1][:, :, None] == jnp.arange(resident_slots, dtype=jnp.int32)
    )
    request_ids = jnp.arange(tables.shape[0], dtype=jnp.int32)
    owner_of = jnp.sum(jnp.where(held_here, request_ids[:, None, None], 0), axis=(0, 1))
    length = lax.dynamic_index_in_dim(lengths, inst_index, 0, keepdims=False)
    own = own_partial(query_rows, section_both, new_kv, length, pair_index, heads, score_scale)

    partials = resident(owner_of, arrived, pool_both, score_scale, query_count)
    parts = lax.all_to_all(partials, "inst", split_axis=0, concat_axis=0, tiled=True)
    lent = arrived[:, : CAP * 2 * half_len].reshape(insts * CAP, 1, 2, half_len, head_dim)
    attended = finish(parts, *own)
    return attended.reshape(queries.shape), lent


def solution(mesh):
    insts, tp = mesh.devices.shape
    paired = Mesh(mesh.devices.reshape(insts, tp // 2, 2), ("inst", "pair", "core"))
    heads = ("pair", "core")
    return jax.shard_map(
        shards,
        mesh=paired,
        in_specs=(
            P("inst", heads),
            P("inst", heads),
            P("inst"),
            P(),
            P(),
            P("inst", None, heads),
            P("inst"),
        ),
        out_specs=(P("inst", None, heads), P("inst", heads)),
        check_vma=False,
    )
```

time: 180 us -> 142 us (0.79)
  blocking collectives: 83 us -> 0 us
  Pallas kernels: 0 us -> 38.7 us
  waiting for transfers between devices: 19 us -> 54.7 us
  starting transfers between devices: 40.9 us -> 19.6 us
  between operations: 0.98 us -> 14.9 us
  other arithmetic: 10.1 us -> 1.43 us
  matrix products: 11.6 us -> 3.58 us
  local copies, waits for them, and re-layouts: 12.6 us -> 8.39 us
    all_gather x1 -> x0, blocking collectives: 83 us -> none  [shards(): everyone = lax.all_gather(group_queries, 'inst', axis=0, tiled=True)]
    pallas_call x0 -> x3, Pallas kernels: none -> 38.7 us  [the longest x1 34.2 us: pack(): pl.pallas_call(pack_kernel, out_shape=jax.ShapeDtypeStruct((insts, CAP *...]
    all_to_all x1, waiting for transfers between devices: 0.01 us -> 29.8 us  [shards(): lax.all_to_all(outgoing, 'inst', split_axis=0, concat_axis=0, tiled=True)]
    all_gather x0 -> x2, waiting for transfers between devices: none -> 15.2 us  [the longest x1 15.2 us: shards(): lax.all_gather(pool.reshape(pool.shape[0], 2, half_len, head_dim), 'core'...]
    all_to_all x3 -> x1, starting transfers between devices: 19.5 us -> 5.99 us  [shards(): lax.all_to_all(partials, 'inst', split_axis=0, concat_axis=0, tiled=True)]
    all_to_all x3 -> x1, waiting for transfers between devices: 17.1 us -> 8.23 us  [shards(): lax.all_to_all(partials, 'inst', split_axis=0, concat_axis=0, tiled=True)]
    ppermute x4 -> x0, starting transfers between devices: 8.15 us -> none  [partner_2(): lax.ppermute(value, axis, [(i, i ^ 1 << distance) for i in range(lax.axis...]
    dot_general x6 -> x4, matrix products: 11.6 us -> 3.58 us  [the longest x1 1.61 us: own_partial(): jnp.einsum('qbnt,bntd->qd', cached_weights.astype(jnp.bfloat16), value_ro...]
  transfers between devices with their start and end apart: 8 -> 4, of which waited for: 5 -> 3; matrix products, arithmetic and copies ran while one was open for 10% -> 6% of each run, Pallas kernels for 0% -> 24%
where the time goes in v1:
time: 142 us; the launch traced here: 141 us
  waiting for transfers between devices  54.7 us (39%)
  Pallas kernels  38.7 us (27%)
  starting transfers between devices  19.6 us (14%)
  between operations  14.9 us (10%)
  local copies, waits for them, and re-layouts  8.39 us (6%)
  matrix products  3.58 us (3%)
  other arithmetic  1.43 us (1%)
    pallas_call x1, Pallas kernels, pack(): pl.pallas_call(pack_kernel, out_shape=jax.ShapeDtypeStruct((insts, CAP *...  34.2 us
    all_to_all x1, waiting for transfers between devices, shards(): lax.all_to_all(outgoing, 'inst', split_axis=0, concat_axis=0, tiled=True)  29.8 us
    all_gather x1, waiting for transfers between devices, shards(): lax.all_gather(pool.reshape(pool.shape[0], 2, half_len, head_dim), 'core'...  15.2 us
    all_to_all x1, starting transfers between devices, shards(): lax.all_to_all(outgoing, 'inst', split_axis=0, concat_axis=0, tiled=True)  13.5 us
    all_to_all x1, waiting for transfers between devices, shards(): lax.all_to_all(partials, 'inst', split_axis=0, concat_axis=0, tiled=True)  8.23 us
    all_to_all x1, starting transfers between devices, shards(): lax.all_to_all(partials, 'inst', split_axis=0, concat_axis=0, tiled=True)  5.99 us
    unnamed x15, local copies, waits for them, and re-layouts  3.09 us
  transfers between devices with their start and end apart: 4, of which 3 were waited for; matrix products, arithmetic and copies ran while one was open for 6% of the time, Pallas kernels for 24%

profile of v1, /device:TPU:56, one launch (start us, length us, event | category | flops | bytes accessed | tf_op | source)
XLA Modules:
  0.0 141.3 jit_solution(10456411703373118686)
XLA Ops:
  7.2 0.0 copy-start
  7.2 0.0 all-gather.7.cloned.1.call-start
  7.2 0.7 all-gather.7.cloned.1.call-update
  7.9 34.2 %pack.1 = bf16[32,272,128]{2,1,0:T(8,128)(2,1)} custom-call(s32[32]{0:T(128)} %spill_ref.1, bf16[32,128,128]{2,1,0:T(8,128)(2,1)} %bitcast.49, bf16[16,128]{1,0:T(8,128)(2,1)} %bitcast.54), custom_call_target="tpu_custom_call" | custom-call | tf_op jit(solution)/shard_map/pack/pallas_call | solution.py:62
  42.1 0.0 copy-start.6
  42.1 0.0 copy-start.4
  42.1 0.0 copy-start.5
  42.1 13.5 %all-to-all-start = ((bf16[32,272,128]{2,1,0:T(8,128)(2,1)}), bf16[32,272,128]{2,1,0:T(8,128)(2,1)S(1)}, u32[]{:S(2)}, u32[]{:S(2)}) async-start(bf16[32,272,128]{2,1,0:T(8,128)(2,1)} %pack.1), calls=%async_computation | async-start | bytes 4456448 | tf_op jit(solution)/shard_map/all_to_all | solution.py:220
  55.7 0.0 all-gather.5.cloned.1.call-start
  55.7 0.7 all-gather.5.cloned.1.call-update
  56.4 0.0 copy-done.6
  56.4 0.6 dynamic_slice.7
  57.7 0.0 copy-done
  57.8 0.0 copy-done.4
  57.8 0.3 select_reduce_fusion.owner_ref
  58.1 0.1 broadcast_add_fusion
  58.2 0.0 copy-done.5
  58.2 0.1 fusion.25
  58.3 0.7 add_compare_fusion
  59.1 0.0 all-gather.7.cloned.1.call-done
  59.1 1.8 %copy.18 = bf16[64,1,2,64,128]{4,3,0,2,1:T(8,128)(2,1)S(1)} copy(bf16[64,1,2,64,128]{4,3,2,1,0:T(8,128)(2,1)} %all-gather.7.cloned.1.call-done) | data formatting | bytes 4194304 | tf_op jit(solution)/shard_map/all_gather | solution.py:223
  60.8 0.0 copy-start.2
  60.9 1.3 copy-done.2
  62.2 1.0 fusion.24
  63.2 0.3 fusion.4
  63.5 15.2 %all-gather.5.cloned.1.call-done = bf16[80,1,2,64,128]{4,3,2,1,0:T(8,128)(2,1)} async-done(((bf16[40,1,2,64,128]{4,3,2,1,0:T(8,128)(2,1)}), bf16[80,1,2,64,128]{4,3,2,1,0:T(8,128)(2,1)}) %all-gather.5.cloned.1.call-update) | async-done | bytes 2621456 | tf_op jit(solution)/shard_map/all_gather | solution.py:222
  78.7 29.8 %all-to-all-done.arrived_ref = bf16[32,272,128]{2,1,0:T(8,128)(2,1)S(1)} async-done(((bf16[32,272,128]{2,1,0:T(8,128)(2,1)}), bf16[32,272,128]{2,1,0:T(8,128)(2,1)S(1)}, u32[]{:S(2)}, u32[]{:S(2)}) %all-to-all-start) | async-done | bytes 2228256 | tf_op jit(solution)/shard_map/all_to_all | solution.py:220
  108.6 0.0 copy-start.1
  108.6 1.7 %copy-done.1 = bf16[80,1,2,64,128]{4,3,2,1,0:T(8,128)(2,1)S(1)} copy-done((bf16[80,1,2,64,128]{4,3,2,1,0:T(8,128)(2,1)S(1)}, bf16[80,1,2,64,128]{4,3,2,1,0:T(8,128)(2,1)}, u32[]{:S(2)}) %copy-start.1) | copy-done | bytes 2621464
  110.3 2.8 %resident.1 = bf16[32,32,128]{2,1,0:T(8,128)(2,1)} custom-call(s32[40]{0:T(128)S(1)} %select_reduce_fusion.owner_ref, bf16[32,272,128]{2,1,0:T(8,128)(2,1)S(1)} %all-to-all-done.arrived_ref, bf16[2,40,2,64,128]{4,3,2,1,0:T(8,128)(2,1)S(1)} %bitcast.46), custom_call_target="tpu_custom_call" | custom-call | tf_op jit(solution)/shard_map/resident/pallas_call | solution.py:128
  113.1 6.0 %all-to-all-start.1 = ((bf16[32,32,128]{2,1,0:T(8,128)(2,1)}), bf16[32,32,128]{2,1,0:T(8,128)(2,1)S(1)}, u32[]{:S(2)}, u32[]{:S(2)}) async-start(bf16[32,32,128]{2,1,0:T(8,128)(2,1)} %resident.1), calls=%async_computation.1 | async-start | bytes 524288 | tf_op jit(solution)/shard_map/all_to_all | solution.py:233
  119.1 1.6 %convolution_bitcast_fusion = f32[16,128]{1,0:T(8,128)S(1)} fusion(bf16[2,32,2,64,128]{4,3,1,0,2:T(8,128)(2,1)} %bitcast.48, f32[16,2,32,64]{3,0,2,1:T(8,128)S(1)} %get-tuple-element.15, f32[16]{0:T(128)S(1)} %max.11, pred[2,32,64]{2,1,0:T(8,128)(4,1)S(1)} %add_compare_fusion), kind=kOutput, calls=%fused_computation.3 | convolution fusion | flops 16973824 | bytes 1323072 | tf_op jit(solution)/shard_map/qbnt,bntd->qd/dot_general | solution.py:201
  120.7 0.8 convolution_add_fusion.mix_ref
  121.5 1.6 %slice.32 = bf16[32,256,128]{2,1,0:T(8,128)(2,1)} slice(bf16[32,272,128]{2,1,0:T(8,128)(2,1)S(1)} %all-to-all-done.arrived_ref), slice={[0:32], [0:256], [0:128]} | slice | bytes 4194304 | tf_op jit(solution)/shard_map/slice | solution.py:234
  123.1 8.2 %all-to-all-done.1.parts_ref = bf16[32,32,128]{2,1,0:T(8,128)(2,1)S(1)} async-done(((bf16[32,32,128]{2,1,0:T(8,128)(2,1)}), bf16[32,32,128]{2,1,0:T(8,128)(2,1)S(1)}, u32[]{:S(2)}, u32[]{:S(2)}) %all-to-all-start.1) | async-done | bytes 262176 | tf_op jit(solution)/shard_map/all_to_all | solution.py:233
  131.3 0.0 copy-start.3
  131.3 0.7 broadcast_in_dim.65.total_ref
  132.0 0.7 broadcast_in_dim.66.top_ref
  132.7 0.0 copy-done.3
  132.7 1.8 %finish.1 = bf16[16,128]{1,0:T(8,128)(2,1)} custom-call(bf16[32,32,128]{2,1,0:T(8,128)(2,1)} %copy-done.3, f32[16,128]{1,0:T(8,128)} %convolution_add_fusion.mix_ref, f32[16,128]{1,0:T(8,128)} %broadcast_in_dim.65.total_ref, f32[16,128]{1,0:T(8,128)} %broadcast_in_dim.66.top_ref), custom_call_target="tpu_custom_call" | custom-call | tf_op jit(solution)/shard_map/finish/pallas_call | solution.py:165
  (11 shorter events, 0.1 us)
Async XLA Ops:
  7.2 50.5 %copy-start = (bf16[1,4,2,8,128]{4,3,2,1,0:T(8,128)(2,1)S(1)}, bf16[1,4,2,8,128]{4,3,2,1,0:T(8,128)(2,1)}, u32[]{:S(2)}) copy-start(bf16[1,4,2,8,128]{4,3,2,1,0:T(8,128)(2,1)} %param.13) | copy-start | bytes 49156
  7.2 51.9 %all-gather.7.cloned.1.call-start = ((), (), s32[]{:S(2)}) async-start(), calls=%async_computation.3 | async-start | bytes 3145728 | tf_op jit(solution)/shard_map/all_gather | solution.py:223
  42.1 14.3 %copy-start.6 = (s32[32]{0:T(128)S(1)}, s32[32]{0:T(128)}, u32[]{:S(2)}) copy-start(s32[32]{0:T(128)} %param.11) | copy-start | bytes 388
  42.1 15.7 %copy-start.4 = (s32[32,111,2]{1,2,0:T(2,128)S(1)}, s32[32,111,2]{1,2,0:T(2,128)}, u32[]{:S(2)}) copy-start(s32[32,111,2]{1,2,0:T(2,128)} %param.10) | copy-start | bytes 85252
  42.1 16.1 %copy-start.5 = (bf16[1,4,4,128]{3,2,1,0:T(4,128)(2,1)S(1)}, bf16[1,4,4,128]{3,2,1,0:T(4,128)(2,1)}, u32[]{:S(2)}) copy-start(bf16[1,4,4,128]{3,2,1,0:T(4,128)(2,1)} %param.12) | copy-start | bytes 12292
  42.1 66.5 %all-to-all-start = ((bf16[32,272,128]{2,1,0:T(8,128)(2,1)}), bf16[32,272,128]{2,1,0:T(8,128)(2,1)S(1)}, u32[]{:S(2)}, u32[]{:S(2)}) async-start(bf16[32,272,128]{2,1,0:T(8,128)(2,1)} %pack.1), calls=%async_computation | async-start | bytes 4456448 | tf_op jit(solution)/shard_map/all_to_all | solution.py:220
  55.7 23.1 %all-gather.5.cloned.1.call-start = ((), (), s32[]{:S(2)}) async-start(), calls=%async_computation.2 | async-start | bytes 3932160 | tf_op jit(solution)/shard_map/all_gather | solution.py:222
  60.8 1.3 copy-start.2
  108.6 1.7 %copy-start.1 = (bf16[80,1,2,64,128]{4,3,2,1,0:T(8,128)(2,1)S(1)}, bf16[80,1,2,64,128]{4,3,2,1,0:T(8,128)(2,1)}, u32[]{:S(2)}) copy-start(bf16[80,1,2,64,128]{4,3,2,1,0:T(8,128)(2,1)} %all-gather.5.cloned.1.call-done) | copy-start | bytes 7864324
  113.1 18.2 %all-to-all-start.1 = ((bf16[32,32,128]{2,1,0:T(8,128)(2,1)}), bf16[32,32,128]{2,1,0:T(8,128)(2,1)S(1)}, u32[]{:S(2)}, u32[]{:S(2)}) async-start(bf16[32,32,128]{2,1,0:T(8,128)(2,1)} %resident.1), calls=%async_computation.1 | async-start | bytes 524288 | tf_op jit(solution)/shard_map/all_to_all | solution.py:233
  131.3 1.3 copy-start.3
Sparse Core Ops, SparseCore 0:
  10.1 22.7 all-gather.6
  58.6 20.1 all-gather.4

commit v2 on v1

v2 whole, which is shorter than its diff:
```python
import functools

import jax
import jax.numpy as jnp
from jax import lax
from jax.experimental import pallas as pl
from jax.experimental.pallas import tpu as pltpu
from jax.sharding import Mesh, PartitionSpec as P

PAGE = 128
CAP = 2
NEG = -1e30
NEW = 4
STAT_ROWS = 8
LENT_COPIES = 8
MIB = 1024 * 1024
NT = (((1,), (1,)), ((), ()))


def in_vmem(value):
    return pltpu.with_memory_space_constraint(value, pltpu.VMEM)


def in_hbm(value):
    return pltpu.with_memory_space_constraint(value, pltpu.HBM)


def plan_kernel(spill_ref, owner_ref, out_ref):
    sectioned, slots = spill_ref.shape[0], owner_ref.shape[0]
    insts = (out_ref.shape[0] - slots - sectioned) // (CAP + 1)
    empty, count = slots + sectioned, slots + sectioned + CAP * insts
    for slot in range(slots):
        out_ref[slot] = owner_ref[slot]
    for dest in range(insts):
        out_ref[count + dest] = 0
    for row in range(sectioned):
        dest = spill_ref[row]
        rank = out_ref[count + dest]
        out_ref[count + dest] = rank + 1
        out_ref[slots + row] = dest * CAP + rank
    found = jnp.int32(0)
    for dest in range(insts):
        filled = out_ref[count + dest]
        for rank in range(CAP):
            out_ref[empty + found] = dest * CAP + rank
            found = found + (filled <= rank).astype(jnp.int32)


def plan(spill_to, owner_of, insts):
    length = owner_of.shape[0] + spill_to.shape[0] + (CAP + 1) * insts
    return pl.pallas_call(
        plan_kernel,
        out_shape=pltpu.SMEM((length,), jnp.int32),
        in_specs=[pl.BlockSpec(memory_space=pltpu.SMEM)] * 2,
        out_specs=pl.BlockSpec(memory_space=pltpu.SMEM),
        compiler_params=pltpu.CompilerParams(vmem_limit_bytes=MIB),
        cost_estimate=pl.CostEstimate(flops=10**11, bytes_accessed=10**8, transcendentals=0),
        name="plan",
    )(in_hbm(spill_to), owner_of)


def resident_kernel(
    score_scale,
    plan_ref,
    asked_ref,
    near_ref,
    far_ref,
    section_ref,
    out_ref,
    pages,
    zeros,
    partials,
    score,
    top,
    total,
    mix,
    page_sem,
    slot_sem,
    part_sem,
):
    requests, query_count = mix.shape[0], mix.shape[1]
    slots = near_ref.shape[0]
    sectioned, rows = section_ref.shape[0], section_ref.shape[1]
    page_copy = pltpu.make_async_copy(section_ref, pages, page_sem)
    page_copy.start()
    zeros[...] = jnp.zeros_like(zeros)
    top[...] = jnp.full(top.shape, NEG, jnp.float32)
    total[...] = jnp.zeros_like(total)
    mix[...] = jnp.zeros_like(mix)

    def slot_copy(source, place):
        start = pl.multiple_of(lax.rem(place, CAP) * rows, rows)
        return pltpu.make_async_copy(source, out_ref.at[lax.div(place, CAP), pl.ds(start, rows)], slot_sem)

    for slot in range(slots):
        owner = plan_ref[slot]
        keys = jnp.concatenate([near_ref[slot, 0], far_ref[slot, 0]], axis=0)
        found = lax.dot_general(asked_ref[owner], keys, NT, preferred_element_type=jnp.float32) * score_scale
        score[slot] = found
        top[owner] = jnp.maximum(top[owner], found)

    page_copy.wait()

    @pl.loop(0, sectioned)
    def _(row):
        slot_copy(pages.at[row], plan_ref[slots + row]).start()

    @pl.loop(0, CAP * requests - sectioned)
    def _(row):
        slot_copy(zeros, plan_ref[slots + sectioned + row]).start()

    for request in range(requests):
        top[request] = jnp.broadcast_to(jnp.max(top[request], axis=1, keepdims=True), top.shape[1:])
    for slot in range(slots):
        owner = plan_ref[slot]
        weights = jnp.exp(score[slot] - top[owner])
        values = jnp.concatenate([near_ref[slot, 1], far_ref[slot, 1]], axis=0)
        total[owner] = total[owner] + weights
        mix[owner] = mix[owner] + jnp.dot(
            weights.astype(jnp.bfloat16), values, preferred_element_type=jnp.float32
        )
    gap = lax.broadcasted_iota(jnp.int32, top.shape[1:], 1) - lax.broadcasted_iota(jnp.int32, top.shape[1:], 0)
    stat_rows = partials.shape[1] - query_count
    for request in range(requests):
        norm = jnp.sum(total[request], axis=1, keepdims=True)
        held = norm > 0.0
        safe = jnp.where(held, norm, 1.0)
        partials[request, 0:query_count] = (mix[request] / safe).astype(jnp.bfloat16)
        level = jnp.where(held, top[request] + jnp.log(safe), NEG)
        high = level.astype(jnp.bfloat16).astype(jnp.float32)
        middle = (level - high).astype(jnp.bfloat16).astype(jnp.float32)
        low = level - high - middle
        terms = jnp.where(
            gap == 0, high, jnp.where(gap == query_count, middle, jnp.where(gap == 2 * query_count, low, 0.0))
        )
        terms = jnp.sum(terms, axis=0, keepdims=True)
        partials[request, query_count:] = jnp.broadcast_to(terms, (stat_rows, terms.shape[1])).astype(jnp.bfloat16)
    part_copy = pltpu.make_async_copy(partials, out_ref.at[:, pl.ds(CAP * rows, partials.shape[1])], part_sem)
    part_copy.start()
    part_copy.wait()
    all_slots = out_ref.at[:, pl.ds(0, CAP * rows)]
    pltpu.make_async_copy(all_slots, all_slots, slot_sem).wait()


def resident(steps_plan, asked, near, far, section_pages, score_scale):
    requests, query_count, head_dim = asked.shape
    slots = near.shape[0]
    tokens = 2 * near.shape[2]
    rows = section_pages.shape[1]
    part_rows = query_count + STAT_ROWS
    return pl.pallas_call(
        functools.partial(resident_kernel, score_scale),
        out_shape=pltpu.HBM((requests, CAP * rows + part_rows, head_dim), asked.dtype),
        in_specs=[
            pl.BlockSpec(memory_space=pltpu.SMEM),
            pl.BlockSpec(memory_space=pltpu.VMEM),
            pl.BlockSpec(memory_space=pltpu.VMEM),
            pl.BlockSpec(memory_space=pltpu.VMEM),
            pl.BlockSpec(memory_space=pl.ANY),
        ],
        out_specs=pl.BlockSpec(memory_space=pl.ANY),
        scratch_shapes=[
            pltpu.VMEM(section_pages.shape, section_pages.dtype),
            pltpu.VMEM(section_pages.shape[1:], section_pages.dtype),
            pltpu.VMEM((requests, part_rows, head_dim), asked.dtype),
            pltpu.VMEM((slots, query_count, tokens), jnp.float32),
            pltpu.VMEM((requests, query_count, tokens), jnp.float32),
            pltpu.VMEM((requests, query_count, tokens), jnp.float32),
            pltpu.VMEM((requests, query_count, head_dim), jnp.float32),
            pltpu.SemaphoreType.DMA,
            pltpu.SemaphoreType.DMA,
            pltpu.SemaphoreType.DMA,
        ],
        compiler_params=pltpu.CompilerParams(vmem_limit_bytes=16 * MIB),
        name="resident",
    )(steps_plan, in_vmem(asked), in_vmem(near), in_vmem(far), in_hbm(section_pages))


def own_kernel(score_scale, place_ref, query_ref, near_ref, far_ref, fresh_ref, out_ref):
    length, near_half = place_ref[0], place_ref[1]
    query_rows = query_ref[...]
    query_count, head_dim = query_rows.shape
    sectioned, half_len = near_ref.shape[0], near_ref.shape[2]
    first_page = (length + PAGE - 1) // PAGE - sectioned
    column = lax.broadcasted_iota(jnp.int32, (query_count, sectioned * half_len), 1)
    base = first_page * PAGE + column // half_len * PAGE + column % half_len
    scores, masks = [], []
    for half_ref, half in ((near_ref, near_half), (far_ref, 1 - near_half)):
        keys = half_ref[:, 0].reshape(sectioned * half_len, head_dim)
        found = lax.dot_general(query_rows, keys, NT, preferred_element_type=jnp.float32) * score_scale
        masks.append(base + half * half_len < length)
        scores.append(found)
    found = lax.dot_general(query_rows, fresh_ref[0], NT, preferred_element_type=jnp.float32) * score_scale
    step = lax.broadcasted_iota(jnp.int32, found.shape, 0) // (query_count // NEW)
    token = lax.broadcasted_iota(jnp.int32, found.shape, 1)
    masks.append(token <= step)
    scores.append(found)
    scores = [jnp.where(mask, found, NEG) for mask, found in zip(masks, scores, strict=True)]
    top = functools.reduce(jnp.maximum, [jnp.max(found, axis=1, keepdims=True) for found in scores])
    weights = [jnp.where(mask, jnp.exp(found - top), 0.0) for mask, found in zip(masks, scores, strict=True)]
    total = sum(jnp.sum(weight, axis=1, keepdims=True) for weight in weights)
    values = [
        near_ref[:, 1].reshape(sectioned * half_len, head_dim),
        far_ref[:, 1].reshape(sectioned * half_len, head_dim),
        fresh_ref[1],
    ]
    out_ref[0] = sum(
        jnp.dot(weight.astype(jnp.bfloat16), value, preferred_element_type=jnp.float32)
        for weight, value in zip(weights, values, strict=True)
    )
    out_ref[1] = jnp.broadcast_to(total, (query_count, head_dim))
    out_ref[2] = jnp.broadcast_to(top, (query_count, head_dim))


def own_partial(place, query_rows, near, far, fresh, score_scale):
    return pl.pallas_call(
        functools.partial(own_kernel, score_scale),
        out_shape=jax.ShapeDtypeStruct((3,) + query_rows.shape, jnp.float32),
        in_specs=[pl.BlockSpec(memory_space=pltpu.SMEM)] + [pl.BlockSpec(memory_space=pltpu.VMEM)] * 4,
        out_specs=pl.BlockSpec(memory_space=pltpu.VMEM),
        compiler_params=pltpu.CompilerParams(vmem_limit_bytes=16 * MIB),
        name="own_pages",
    )(place, query_rows, near, far, fresh)


def finish_kernel(arrived_ref, own_ref, out_ref, lent_ref, own, lent_sems, own_sem):
    insts, page_rows = lent_ref.shape[0], lent_ref.shape[1]
    query_count, head_dim = out_ref.shape
    pieces = lent_sems.shape[0]
    own_copy = pltpu.make_async_copy(own_ref, own, own_sem)
    own_copy.start()
    lent_copies = []
    for piece in range(pieces):
        part = pl.ds(piece * (insts // pieces), insts // pieces)
        lent_copies.append(
            pltpu.make_async_copy(
                arrived_ref.at[part, pl.ds(0, page_rows)], lent_ref.at[part], lent_sems.at[piece]
            )
        )
        lent_copies[-1].start()
    outs = arrived_ref[:, page_rows : page_rows + query_count].astype(jnp.float32)
    terms = arrived_ref[:, page_rows + query_count :].astype(jnp.float32)[:, 0:1]
    shape = (query_count, head_dim)
    lane = lax.broadcasted_iota(jnp.int32, shape, 1)
    own_lane = (lane % query_count == lax.broadcasted_iota(jnp.int32, shape, 0)) & (lane < 3 * query_count)
    levels = jnp.sum(jnp.where(own_lane[None], terms, 0.0), axis=2, keepdims=True)
    own_copy.wait()
    own_mix, own_total, own_top = own[0], own[1], own[2]
    joint = jnp.maximum(jnp.max(levels, axis=0), own_top)
    factor = jnp.exp(levels - joint[None])
    own_factor = jnp.exp(own_top - joint)
    norm = jnp.sum(factor, axis=0) + own_total * own_factor
    mixture = jnp.sum(outs * factor, axis=0) + own_mix * own_factor
    out_ref[...] = (mixture / norm).astype(jnp.bfloat16)
    for copy in lent_copies:
        copy.wait()


def finish(arrived, own, page_rows):
    insts, head_dim = arrived.shape[0], arrived.shape[2]
    return pl.pallas_call(
        finish_kernel,
        out_shape=(
            jax.ShapeDtypeStruct(own.shape[1:], jnp.bfloat16),
            pltpu.HBM((insts, page_rows, head_dim), arrived.dtype),
        ),
        in_specs=[pl.BlockSpec(memory_space=pltpu.VMEM), pl.BlockSpec(memory_space=pl.ANY)],
        out_specs=(pl.BlockSpec(memory_space=pltpu.VMEM), pl.BlockSpec(memory_space=pl.ANY)),
        scratch_shapes=[
            pltpu.VMEM(own.shape, own.dtype),
            pltpu.SemaphoreType.DMA((LENT_COPIES,)),
            pltpu.SemaphoreType.DMA,
        ],
        compiler_params=pltpu.CompilerParams(vmem_limit_bytes=8 * MIB),
        name="finish",
    )(in_vmem(arrived), in_hbm(own))


def shards(pool, sectioning, spill_to, tables, lengths, queries, new_kv):
    insts = lax.axis_size("inst")
    inst_index = lax.axis_index("inst")
    pair_index = lax.axis_index("pair")
    core = lax.axis_index("core")
    resident_slots, half_len, head_dim = pool.shape[0], pool.shape[3], pool.shape[4]
    sectioned = sectioning.shape[0]
    steps = queries.shape[1]
    query_count = steps * queries.shape[2]
    score_scale = head_dim ** (-0.5)
    query_rows = queries.reshape(query_count, head_dim)

    spread = jnp.broadcast_to(query_rows[None], (insts,) + query_rows.shape)
    asked = lax.all_to_all(spread, "inst", split_axis=0, concat_axis=0, tiled=True)

    section_pages = sectioning.reshape(sectioned, 2 * half_len, head_dim)
    near_pool = pool.reshape(resident_slots, 2, half_len, head_dim)
    near_section = sectioning.reshape(sectioned, 2, half_len, head_dim)
    far_pool = lax.ppermute(near_pool, "core", [(0, 1), (1, 0)])
    far_section = lax.ppermute(near_section, "core", [(0, 1), (1, 0)])
    held_here = (tables[:, :, 0] == inst_index)[:, :, None] & (
        tables[:, :, 1][:, :, None] == jnp.arange(resident_slots, dtype=jnp.int32)
    )
    request_ids = jnp.arange(tables.shape[0], dtype=jnp.int32)
    owner_of = jnp.sum(jnp.where(held_here, request_ids[:, None, None], 0), axis=(0, 1))
    length = lax.dynamic_index_in_dim(lengths, inst_index, 0, keepdims=False)
    place = jnp.stack([length, core.astype(jnp.int32)])
    fresh = lax.dynamic_slice_in_dim(new_kv[0], pair_index, 1, 2)[:, :, 0]
    fresh = jnp.pad(jnp.swapaxes(fresh, 0, 1), ((0, 0), (0, query_count - steps), (0, 0)))
    own = own_partial(place, query_rows, near_section, far_section, fresh, score_scale)

    steps_plan = plan(spill_to, owner_of, insts)
    outgoing = resident(steps_plan, asked, near_pool, far_pool, section_pages, score_scale)
    arrived = lax.all_to_all(outgoing, "inst", split_axis=0, concat_axis=0, tiled=True)
    attended, lent = finish(arrived, own, CAP * 2 * half_len)
    return attended.reshape(queries.shape), lent.reshape(insts * CAP, 1, 2, half_len, head_dim)


def solution(mesh):
    insts, tp = mesh.devices.shape
    paired = Mesh(mesh.devices.reshape(insts, tp // 2, 2), ("inst", "pair", "core"))
    heads = ("pair", "core")
    return jax.shard_map(
        shards,
        mesh=paired,
        in_specs=(
            P("inst", heads),
            P("inst", heads),
            P("inst"),
            P(),
            P(),
            P("inst", None, heads),
            P("inst"),
        ),
        out_specs=(P("inst", None, heads), P("inst", heads)),
        check_vma=False,
    )
```

time: 142 us -> 91.3 us (0.64)
  Pallas kernels: 38.7 us -> 8.98 us
  between operations: 14.9 us -> 0.8 us
  local copies, waits for them, and re-layouts: 8.39 us -> 3.47 us
  matrix products: 3.58 us -> 0 us
  starting transfers between devices: 19.6 us -> 21.6 us
    pallas_call x2 -> x3, Pallas kernels: 36 us -> 5.19 us  [the longest x1 1.99 us: finish(): pl.pallas_call(finish_kernel, out_shape=(jax.ShapeDtypeStruct(own.shape[1...]
    all_to_all x1, waiting for transfers between devices: 29.8 us -> 47.3 us  [shards(): lax.all_to_all(outgoing, 'inst', split_axis=0, concat_axis=0, tiled=True)]
    all_gather x2 -> x0, waiting for transfers between devices: 15.2 us -> none  [the longest x1 15.2 us: shards(): lax.all_gather(pool.reshape(pool.shape[0], 2, half_len, head_dim), 'core'...]
    all_to_all x1, starting transfers between devices: 13.5 us -> 4.6 us  [shards(): lax.all_to_all(outgoing, 'inst', split_axis=0, concat_axis=0, tiled=True)]
    all_to_all x1, starting transfers between devices: 5.99 us -> 13.2 us  [shards(): lax.all_to_all(spread, 'inst', split_axis=0, concat_axis=0, tiled=True)]
    ppermute x0 -> x2, starting transfers between devices: none -> 3.84 us  [the longest x1 1.92 us: shards(): far_pool = lax.ppermute(near_pool, 'core', [(0, 1), (1, 0)])]
    dot_general x4 -> x0, matrix products: 3.58 us -> none  [the longest x1 1.61 us: own_partial(): jnp.einsum('qbnt,bntd->qd', cached_weights.astype(jnp.bfloat16), value_ro...]
    unnamed x15 -> x12, local copies, waits for them, and re-layouts: 3.09 us -> 0.63 us
  transfers between devices with their start and end apart: 4 -> 4, of which waited for: 3 -> 3; matrix products, arithmetic and copies ran while one was open for 6% -> 3% of each run, Pallas kernels for 24% -> 4%
where the time goes in v2:
time: 91.3 us; the launch traced here: 90.7 us
  waiting for transfers between devices  54.8 us (60%)
  starting transfers between devices  21.6 us (24%)
  Pallas kernels  8.98 us (10%)
  local copies, waits for them, and re-layouts  3.47 us (4%)
  other arithmetic  0.99 us (1%)
    all_to_all x1, waiting for transfers between devices, shards(): lax.all_to_all(outgoing, 'inst', split_axis=0, concat_axis=0, tiled=True)  47.3 us
    all_to_all x1, starting transfers between devices, shards(): lax.all_to_all(spread, 'inst', split_axis=0, concat_axis=0, tiled=True)  13.2 us
    all_to_all x1, waiting for transfers between devices, shards(): lax.all_to_all(spread, 'inst', split_axis=0, concat_axis=0, tiled=True)  6.12 us
    all_to_all x1, starting transfers between devices, shards(): lax.all_to_all(outgoing, 'inst', split_axis=0, concat_axis=0, tiled=True)  4.6 us
    pallas_call x1, Pallas kernels, resident(): pl.pallas_call(functools.partial(resident_kernel, score_scale), out_shape...  3.79 us
    pallas_call x1, Pallas kernels, finish(): pl.pallas_call(finish_kernel, out_shape=(jax.ShapeDtypeStruct(own.shape[1...  1.99 us
    pallas_call x1, Pallas kernels, own_partial(): pl.pallas_call(functools.partial(own_kernel, score_scale), out_shape=jax....  1.97 us
    ppermute x1, starting transfers between devices, shards(): far_pool = lax.ppermute(near_pool, 'core', [(0, 1), (1, 0)])  1.92 us
  transfers between devices with their start and end apart: 4, of which 3 were waited for; matrix products, arithmetic and copies ran while one was open for 3% of the time, Pallas kernels for 4%

profile of v2, /device:TPU:56, one launch (start us, length us, event | category | flops | bytes accessed | tf_op | source)
XLA Modules:
  0.0 90.7 jit_solution(2423937120841140984)
XLA Ops:
  0.6 0.0 copy-start
  0.6 1.4 %broadcast_in_dim.25 = bf16[32,16,128]{2,1,0:T(8,128)(2,1)} broadcast(bf16[16,128]{1,0:T(8,128)(2,1)} %bitcast.23), dimensions={1,2} | broadcast | bytes 135168 | tf_op jit(solution)/shard_map/broadcast_in_dim | solution.py:291
  2.0 13.2 %all-to-all-start = ((bf16[32,16,128]{2,1,0:T(8,128)(2,1)}), bf16[32,16,128]{2,1,0:T(8,128)(2,1)S(1)}, u32[]{:S(2)}, u32[]{:S(2)}) async-start(bf16[32,16,128]{2,1,0:T(8,128)(2,1)} %broadcast_in_dim.25), calls=%async_computation | async-start | bytes 262144 | tf_op jit(solution)/shard_map/all_to_all | solution.py:292
  15.2 1.9 %collective-permute-start = (bf16[40,2,64,128]{3,2,1,0:T(8,128)(2,1)}, bf16[40,2,64,128]{3,2,1,0:T(8,128)(2,1)S(1)}, u32[]{:S(2)}, u32[]{:S(2)}) collective-permute-start(bf16[40,2,64,128]{3,2,1,0:T(8,128)(2,1)} %bitcast.21), channel_id=1, source_target_pairs={{0,1},{1,0},{2,3},{3,2},{4,5},{5,4},{6,7},{7,6},{8,9},{9,8},{10,11... | collective-permute-start | bytes 3932168 | tf_op jit(solution)/shard_map/ppermute | solution.py:297
  17.1 0.9 fusion.1
  18.0 0.3 select_reduce_fusion.owner_ref
  18.3 0.0 copy-start.2
  18.3 1.2 %plan.1.plan_ref = s32[168]{0:T(256)S(4)} custom-call(s32[32]{0:T(128)} %spill_ref.1, s32[40]{0:T(128)S(1)} %select_reduce_fusion.owner_ref), custom_call_target="tpu_custom_call" | custom-call | flops 99999997952 | bytes 100000000 | tf_op jit(solution)/shard_map/plan/pallas_call | solution.py:51
  19.5 6.1 %all-to-all-done.asked_ref = bf16[32,16,128]{2,1,0:T(8,128)(2,1)S(1)} async-done(((bf16[32,16,128]{2,1,0:T(8,128)(2,1)}), bf16[32,16,128]{2,1,0:T(8,128)(2,1)S(1)}, u32[]{:S(2)}, u32[]{:S(2)}) %all-to-all-start) | async-done | bytes 131104 | tf_op jit(solution)/shard_map/all_to_all | solution.py:292
  25.6 0.0 collective-permute-done.far_ref
  25.6 0.0 copy-done.2
  25.6 3.8 %resident.1 = bf16[32,280,128]{2,1,0:T(8,128)(2,1)} custom-call(s32[168]{0:T(256)S(4)} %plan.1.plan_ref, bf16[32,16,128]{2,1,0:T(8,128)(2,1)S(1)} %all-to-all-done.asked_ref, bf16[40,2,64,128]{3,2,1,0:T(8,128)(2,1)S(1)} %bitcast.22, bf16[40,2,64,128]{3,2,1,0:T(8,128)(2,1)S(1)} %collective-permute-done.far_ref, bf16[32,128,128]{2,1,0:T(8,128)(2,1)} %bitcast.18), custom_call_target="tpu_custom_call" | custom-call | tf_op jit(solution)/shard_map/resident/pallas_call | solution.py:151
  29.4 0.0 copy-start.1
  29.4 0.0 copy-start.5
  29.5 0.0 copy-start.4
  29.5 4.6 %all-to-all-start.1 = ((bf16[32,280,128]{2,1,0:T(8,128)(2,1)}), bf16[32,280,128]{2,1,0:T(8,128)(2,1)S(1)}, u32[]{:S(2)}, u32[]{:S(2)}) async-start(bf16[32,280,128]{2,1,0:T(8,128)(2,1)} %resident.1), calls=%async_computation.1 | async-start | bytes 4587520 | tf_op jit(solution)/shard_map/all_to_all | solution.py:312
  34.1 0.0 copy-done.1
  34.1 1.9 %collective-permute-start.1 = (bf16[32,2,64,128]{3,2,1,0:T(8,128)(2,1)S(1)}, bf16[32,2,64,128]{3,2,1,0:T(8,128)(2,1)}, u32[]{:S(2)}, u32[]{:S(2)}) collective-permute-start(bf16[32,2,64,128]{3,2,1,0:T(8,128)(2,1)S(1)} %bitcast.19), channel_id=1, source_target_pairs={{0,1},{1,0},{2,3},{3,2},{4,5},{5,4},{6,7},{7,6},{8,9},{9,8},{10,11... | collective-permute-start | bytes 3145736 | tf_op jit(solution)/shard_map/ppermute | solution.py:298
  36.0 0.0 copy-done
  36.1 0.0 copy-done.5
  36.1 0.6 dynamic_slice.7
  36.7 0.7 pad_add_fusion.place_ref
  37.4 1.4 %collective-permute-done.1.far_ref = bf16[32,2,64,128]{3,2,1,0:T(8,128)(2,1)} collective-permute-done((bf16[32,2,64,128]{3,2,1,0:T(8,128)(2,1)S(1)}, bf16[32,2,64,128]{3,2,1,0:T(8,128)(2,1)}, u32[]{:S(2)}, u32[]{:S(2)}) %collective-permute-start.1) | collective-permute-done | bytes 1048608 | tf_op jit(solution)/shard_map/ppermute | solution.py:298
  38.8 0.0 copy-done.4
  38.8 2.0 %own_pages.1.own_ref = f32[3,16,128]{2,1,0:T(8,128)S(1)} custom-call(s32[2]{0:T(128)S(1)} %pad_add_fusion.place_ref, bf16[16,128]{1,0:T(8,128)(2,1)S(1)} %bitcast.24, bf16[32,2,64,128]{3,2,1,0:T(8,128)(2,1)S(1)} %bitcast.20, bf16[32,2,64,128]{3,2,1,0:T(8,128)(2,1)} %collective-permute-done.1.far_ref, bf16[2,16,128]{2,1,0:T(8,128)(2,1)S(1)} %pad.4.fresh_ref), custom_call_target="tpu_custom_call" | custom-call | tf_op jit(solution)/shard_map/own_pages/pallas_call | solution.py:216
  40.8 0.0 copy-start.3
  40.8 0.6 copy-done.3
  41.4 47.3 %all-to-all-done.1.arrived_ref = bf16[32,280,128]{2,1,0:T(8,128)(2,1)S(1)} async-done(((bf16[32,280,128]{2,1,0:T(8,128)(2,1)}), bf16[32,280,128]{2,1,0:T(8,128)(2,1)S(1)}, u32[]{:S(2)}, u32[]{:S(2)}) %all-to-all-start.1) | async-done | bytes 2293792 | tf_op jit(solution)/shard_map/all_to_all | solution.py:312
  88.7 2.0 %finish.1 = (bf16[16,128]{1,0:T(8,128)(2,1)}, bf16[32,256,128]{2,1,0:T(8,128)(2,1)}) custom-call(bf16[32,280,128]{2,1,0:T(8,128)(2,1)S(1)} %all-to-all-done.1.arrived_ref, f32[3,16,128]{2,1,0:T(8,128)} %copy-done.3), custom_call_target="tpu_custom_call" | custom-call | tf_op jit(solution)/shard_map/finish/pallas_call | solution.py:261
  (4 shorter events, 0.0 us)
Async XLA Ops:
  0.6 35.4 %copy-start = (bf16[1,4,2,8,128]{4,3,2,1,0:T(8,128)(2,1)S(1)}, bf16[1,4,2,8,128]{4,3,2,1,0:T(8,128)(2,1)}, u32[]{:S(2)}) copy-start(bf16[1,4,2,8,128]{4,3,2,1,0:T(8,128)(2,1)} %param.13) | copy-start | bytes 49156
  2.0 23.6 %all-to-all-start = ((bf16[32,16,128]{2,1,0:T(8,128)(2,1)}), bf16[32,16,128]{2,1,0:T(8,128)(2,1)S(1)}, u32[]{:S(2)}, u32[]{:S(2)}) async-start(bf16[32,16,128]{2,1,0:T(8,128)(2,1)} %broadcast_in_dim.25), calls=%async_computation | async-start | bytes 262144 | tf_op jit(solution)/shard_map/all_to_all | solution.py:292
  15.2 10.5 %collective-permute-start = (bf16[40,2,64,128]{3,2,1,0:T(8,128)(2,1)}, bf16[40,2,64,128]{3,2,1,0:T(8,128)(2,1)S(1)}, u32[]{:S(2)}, u32[]{:S(2)}) collective-permute-start(bf16[40,2,64,128]{3,2,1,0:T(8,128)(2,1)} %bitcast.21), channel_id=1, source_target_pairs={{0,1},{1,0},{2,3},{3,2},{4,5},{5,4},{6,7},{7,6},{8,9},{9,8},{10,11... | collective-permute-start | bytes 3932168 | tf_op jit(solution)/shard_map/ppermute | solution.py:297
  18.3 7.4 %copy-start.2 = (bf16[40,1,2,64,128]{4,3,2,1,0:T(8,128)(2,1)S(1)}, bf16[40,1,2,64,128]{4,3,2,1,0:T(8,128)(2,1)}, u32[]{:S(2)}) copy-start(bf16[40,1,2,64,128]{4,3,2,1,0:T(8,128)(2,1)} %param.7) | copy-start | bytes 3932164
  29.4 4.7 %copy-start.1 = (bf16[32,1,2,64,128]{4,3,2,1,0:T(8,128)(2,1)S(1)}, bf16[32,1,2,64,128]{4,3,2,1,0:T(8,128)(2,1)}, u32[]{:S(2)}) copy-start(bf16[32,1,2,64,128]{4,3,2,1,0:T(8,128)(2,1)} %param.8) | copy-start | bytes 3145732
  29.4 6.6 %copy-start.5 = (s32[32]{0:T(128)S(1)}, s32[32]{0:T(128)}, u32[]{:S(2)}) copy-start(s32[32]{0:T(128)} %param.11) | copy-start | bytes 388
  29.5 9.3 %copy-start.4 = (bf16[1,4,4,128]{3,2,1,0:T(4,128)(2,1)S(1)}, bf16[1,4,4,128]{3,2,1,0:T(4,128)(2,1)}, u32[]{:S(2)}) copy-start(bf16[1,4,4,128]{3,2,1,0:T(4,128)(2,1)} %param.12) | copy-start | bytes 12292
  29.5 59.2 %all-to-all-start.1 = ((bf16[32,280,128]{2,1,0:T(8,128)(2,1)}), bf16[32,280,128]{2,1,0:T(8,128)(2,1)S(1)}, u32[]{:S(2)}, u32[]{:S(2)}) async-start(bf16[32,280,128]{2,1,0:T(8,128)(2,1)} %resident.1), calls=%async_computation.1 | async-start | bytes 4587520 | tf_op jit(solution)/shard_map/all_to_all | solution.py:312
  34.1 4.7 %collective-permute-start.1 = (bf16[32,2,64,128]{3,2,1,0:T(8,128)(2,1)S(1)}, bf16[32,2,64,128]{3,2,1,0:T(8,128)(2,1)}, u32[]{:S(2)}, u32[]{:S(2)}) collective-permute-start(bf16[32,2,64,128]{3,2,1,0:T(8,128)(2,1)S(1)} %bitcast.19), channel_id=1, source_target_pairs={{0,1},{1,0},{2,3},{3,2},{4,5},{5,4},{6,7},{7,6},{8,9},{9,8},{10,11... | collective-permute-start | bytes 3145736 | tf_op jit(solution)/shard_map/ppermute | solution.py:298
  40.8 0.6 copy-start.3

commit v3 on v2

v3 whole, which is shorter than its diff:
```python
import functools

import jax
import jax.numpy as jnp
from jax import lax
from jax.experimental import pallas as pl
from jax.experimental.pallas import tpu as pltpu
from jax.sharding import Mesh, PartitionSpec as P

PAGE = 128
CAP = 2
NEG = -1e30
NEW = 4
STAT_ROWS = 8
MIB = 1024 * 1024
NT = (((1,), (1,)), ((), ()))


def in_vmem(value):
    return pltpu.with_memory_space_constraint(value, pltpu.VMEM)


def in_hbm(value):
    return pltpu.with_memory_space_constraint(value, pltpu.HBM)


def pack_kernel(
    spill_ref,
    section_ref,
    query_ref,
    whole_ref,
    paged_ref,
    asking_ref,
    spill,
    place,
    count,
    pages,
    zeros,
    asked,
    spread,
    sems,
):
    insts = whole_ref.shape[0]
    sectioned, rows = section_ref.shape[0], section_ref.shape[1]
    core = lax.axis_index("core")
    spill_copy = pltpu.make_async_copy(spill_ref, spill, sems.at[0])
    page_copy = pltpu.make_async_copy(section_ref, pages, sems.at[1])
    query_copy = pltpu.make_async_copy(query_ref, asked, sems.at[2])
    spill_copy.start()
    query_copy.start()
    page_copy.start()
    zeros[...] = jnp.zeros_like(zeros)
    for dest in range(insts):
        count[dest] = 0
    spill_copy.wait()

    @pl.loop(0, sectioned)
    def _(row):
        dest = spill[row]
        place[row] = count[dest]
        count[dest] = count[dest] + 1

    def lay_out(out_ref, query_rows_ref):
        def slot_copy(source, dest, rank):
            start = pl.multiple_of(rank * rows, rows)
            return pltpu.make_async_copy(source, out_ref.at[dest, pl.ds(start, rows)], sems.at[3])

        @pl.loop(0, insts)
        def _(dest):
            filled = count[dest]
            for rank in range(CAP):

                @pl.when(filled <= rank)
                def _():
                    slot_copy(zeros, dest, rank).start()

        query_copy.wait()
        spread[...] = jnp.broadcast_to(asked[...][None], spread.shape)
        spread_copy = pltpu.make_async_copy(spread, query_rows_ref, sems.at[4])
        spread_copy.start()
        page_copy.wait()

        @pl.loop(0, sectioned)
        def _(row):
            slot_copy(pages.at[row], spill[row], place[row]).start()

        all_slots = out_ref.at[:, pl.ds(0, CAP * rows)]
        pltpu.make_async_copy(all_slots, all_slots, sems.at[3]).wait()
        spread_copy.wait()

    @pl.when(core == 1)
    def _():
        lay_out(whole_ref, whole_ref.at[:, pl.ds(CAP * rows, asked.shape[0])])

    @pl.when(core == 0)
    def _():
        lay_out(paged_ref, asking_ref)


def pack(spill_to, section_pages, query_rows, insts):
    sectioned, rows, head_dim = section_pages.shape
    dtype = section_pages.dtype
    query_count = query_rows.shape[0]
    return pl.pallas_call(
        pack_kernel,
        out_shape=(
            pltpu.HBM((insts, CAP * rows + query_count, head_dim), dtype),
            pltpu.HBM((insts, CAP * rows + query_count + STAT_ROWS, head_dim), dtype),
            pltpu.HBM((insts, query_count, head_dim), dtype),
        ),
        in_specs=[pl.BlockSpec(memory_space=pl.ANY)] * 3,
        out_specs=[pl.BlockSpec(memory_space=pl.ANY)] * 3,
        scratch_shapes=[
            pltpu.SMEM(spill_to.shape, jnp.int32),
            pltpu.SMEM(spill_to.shape, jnp.int32),
            pltpu.SMEM((insts,), jnp.int32),
            pltpu.VMEM(section_pages.shape, dtype),
            pltpu.VMEM((rows, head_dim), dtype),
            pltpu.VMEM(query_rows.shape, dtype),
            pltpu.VMEM((insts,) + query_rows.shape, dtype),
            pltpu.SemaphoreType.DMA((5,)),
        ],
        compiler_params=pltpu.CompilerParams(vmem_limit_bytes=4 * MIB),
        name="pack",
    )(in_hbm(spill_to), in_hbm(section_pages), in_hbm(query_rows))


def resident_kernel(score_scale, staged, owner_ref, arrived_ref, near_ref, far_ref, *others):
    copies = []
    if staged:
        *others, near, far, sems = others
        for index in range(2):
            for source, target in ((near_ref, near), (far_ref, far)):
                copies.append(
                    pltpu.make_async_copy(source.at[:, index], target.at[:, index], sems.at[len(copies)])
                )
                copies[-1].start()
        near_ref, far_ref = near, far
    out_ref, partials, score, top, total, mix, part_sem = others[-7:]
    requests, query_count = mix.shape[0], mix.shape[1]
    slots = near_ref.shape[0]
    first_query = arrived_ref.shape[1] - query_count
    top[...] = jnp.full(top.shape, NEG, jnp.float32)
    total[...] = jnp.zeros_like(total)
    mix[...] = jnp.zeros_like(mix)

    for copy in copies[:2]:
        copy.wait()
    for slot in range(slots):
        owner = owner_ref[slot]
        keys = jnp.concatenate([near_ref[slot, 0], far_ref[slot, 0]], axis=0)
        found = lax.dot_general(arrived_ref[owner, first_query:], keys, NT, preferred_element_type=jnp.float32) * score_scale
        score[slot] = found
        top[owner] = jnp.maximum(top[owner], found)

    for request in range(requests):
        top[request] = jnp.broadcast_to(jnp.max(top[request], axis=1, keepdims=True), top.shape[1:])
    for copy in copies[2:]:
        copy.wait()
    for slot in range(slots):
        owner = owner_ref[slot]
        weights = jnp.exp(score[slot] - top[owner])
        values = jnp.concatenate([near_ref[slot, 1], far_ref[slot, 1]], axis=0)
        total[owner] = total[owner] + weights
        mix[owner] = mix[owner] + jnp.dot(
            weights.astype(jnp.bfloat16), values, preferred_element_type=jnp.float32
        )
    gap = lax.broadcasted_iota(jnp.int32, top.shape[1:], 1) - lax.broadcasted_iota(jnp.int32, top.shape[1:], 0)
    stat_rows = partials.shape[1] - query_count
    for request in range(requests):
        norm = jnp.sum(total[request], axis=1, keepdims=True)
        held = norm > 0.0
        safe = jnp.where(held, norm, 1.0)
        partials[request, 0:query_count] = (mix[request] / safe).astype(jnp.bfloat16)
        level = jnp.where(held, top[request] + jnp.log(safe), NEG)
        high = level.astype(jnp.bfloat16).astype(jnp.float32)
        middle = (level - high).astype(jnp.bfloat16).astype(jnp.float32)
        low = level - high - middle
        terms = jnp.where(
            gap == 0, high, jnp.where(gap == query_count, middle, jnp.where(gap == 2 * query_count, low, 0.0))
        )
        terms = jnp.sum(terms, axis=0, keepdims=True)
        partials[request, query_count:] = jnp.broadcast_to(terms, (stat_rows, terms.shape[1])).astype(jnp.bfloat16)
    part_rows = partials.shape[1]
    part_copy = pltpu.make_async_copy(
        partials, out_ref.at[:, pl.ds(out_ref.shape[1] - part_rows, part_rows)], part_sem
    )
    part_copy.start()
    part_copy.wait()


def resident(owner_of, arrived, near, far, outgoing, score_scale, query_count):
    requests, head_dim = arrived.shape[0], arrived.shape[2]
    slots, tokens = near.shape[0], 2 * near.shape[2]
    part_rows = query_count + STAT_ROWS
    out_shape, aliases = (requests, part_rows, head_dim), {}
    staged = outgoing is None
    operands = [owner_of, in_vmem(arrived)]
    spaces = [pltpu.SMEM, pltpu.VMEM]
    scratch = [
        pltpu.VMEM((requests, part_rows, head_dim), arrived.dtype),
        pltpu.VMEM((slots, query_count, tokens), jnp.float32),
        pltpu.VMEM((requests, query_count, tokens), jnp.float32),
        pltpu.VMEM((requests, query_count, tokens), jnp.float32),
        pltpu.VMEM((requests, query_count, head_dim), jnp.float32),
        pltpu.SemaphoreType.DMA,
    ]
    if staged:
        operands += [near, far]
        spaces += [pl.ANY] * 2
        scratch += [pltpu.VMEM(near.shape, near.dtype)] * 2 + [pltpu.SemaphoreType.DMA((4,))]
    else:
        out_shape, aliases = outgoing.shape, {4: 0}
        operands += [in_vmem(near), in_vmem(far), in_hbm(outgoing)]
        spaces += [pltpu.VMEM] * 2 + [pl.ANY]
    return pl.pallas_call(
        functools.partial(resident_kernel, score_scale, staged),
        out_shape=pltpu.HBM(out_shape, arrived.dtype),
        in_specs=[pl.BlockSpec(memory_space=space) for space in spaces],
        out_specs=pl.BlockSpec(memory_space=pl.ANY),
        scratch_shapes=scratch,
        input_output_aliases=aliases,
        compiler_params=pltpu.CompilerParams(vmem_limit_bytes=8 * MIB),
        name="resident_staged" if staged else "resident",
    )(*operands)


def own_kernel(score_scale, place_ref, query_ref, near_ref, far_ref, fresh_ref, out_ref):
    length, near_half = place_ref[0], place_ref[1]
    query_rows = query_ref[...]
    query_count, head_dim = query_rows.shape
    sectioned, half_len = near_ref.shape[0], near_ref.shape[2]
    first_page = (length + PAGE - 1) // PAGE - sectioned
    column = lax.broadcasted_iota(jnp.int32, (query_count, sectioned * half_len), 1)
    base = first_page * PAGE + column // half_len * PAGE + column % half_len
    scores, masks = [], []
    for half_ref, half in ((near_ref, near_half), (far_ref, 1 - near_half)):
        keys = half_ref[:, 0].reshape(sectioned * half_len, head_dim)
        found = lax.dot_general(query_rows, keys, NT, preferred_element_type=jnp.float32) * score_scale
        masks.append(base + half * half_len < length)
        scores.append(found)
    found = lax.dot_general(query_rows, fresh_ref[0], NT, preferred_element_type=jnp.float32) * score_scale
    step = lax.broadcasted_iota(jnp.int32, found.shape, 0) // (query_count // NEW)
    token = lax.broadcasted_iota(jnp.int32, found.shape, 1)
    masks.append(token <= step)
    scores.append(found)
    scores = [jnp.where(mask, found, NEG) for mask, found in zip(masks, scores, strict=True)]
    top = functools.reduce(jnp.maximum, [jnp.max(found, axis=1, keepdims=True) for found in scores])
    weights = [jnp.where(mask, jnp.exp(found - top), 0.0) for mask, found in zip(masks, scores, strict=True)]
    total = sum(jnp.sum(weight, axis=1, keepdims=True) for weight in weights)
    values = [
        near_ref[:, 1].reshape(sectioned * half_len, head_dim),
        far_ref[:, 1].reshape(sectioned * half_len, head_dim),
        fresh_ref[1],
    ]
    out_ref[0] = sum(
        jnp.dot(weight.astype(jnp.bfloat16), value, preferred_element_type=jnp.float32)
        for weight, value in zip(weights, values, strict=True)
    )
    out_ref[1] = jnp.broadcast_to(total, (query_count, head_dim))
    out_ref[2] = jnp.broadcast_to(top, (query_count, head_dim))


def own_partial(place, query_rows, near, far, fresh, score_scale):
    return pl.pallas_call(
        functools.partial(own_kernel, score_scale),
        out_shape=jax.ShapeDtypeStruct((3,) + query_rows.shape, jnp.float32),
        in_specs=[pl.BlockSpec(memory_space=pltpu.SMEM)] + [pl.BlockSpec(memory_space=pltpu.VMEM)] * 4,
        out_specs=pl.BlockSpec(memory_space=pltpu.VMEM),
        compiler_params=pltpu.CompilerParams(vmem_limit_bytes=16 * MIB),
        name="own_pages",
    )(place, query_rows, near, far, fresh)


def lend_kernel(arrived_ref, lent_ref, sem):
    lent_copy = pltpu.make_async_copy(arrived_ref.at[:, pl.ds(0, lent_ref.shape[1])], lent_ref, sem)
    lent_copy.start()
    lent_copy.wait()


def lend(arrived, page_rows):
    insts, head_dim = arrived.shape[0], arrived.shape[2]
    return pl.pallas_call(
        lend_kernel,
        out_shape=pltpu.HBM((insts, page_rows, head_dim), arrived.dtype),
        in_specs=[pl.BlockSpec(memory_space=pl.ANY)],
        out_specs=pl.BlockSpec(memory_space=pl.ANY),
        scratch_shapes=[pltpu.SemaphoreType.DMA],
        compiler_params=pltpu.CompilerParams(vmem_limit_bytes=MIB),
        name="lend",
    )(in_vmem(arrived))


def join(arrived_ref, own_ref, out_ref, own, own_sem):
    query_count, head_dim = out_ref.shape
    first_row = arrived_ref.shape[1] - query_count - STAT_ROWS
    own_copy = pltpu.make_async_copy(own_ref, own, own_sem)
    own_copy.start()
    outs = arrived_ref[:, first_row : first_row + query_count].astype(jnp.float32)
    terms = arrived_ref[:, first_row + query_count :].astype(jnp.float32)[:, 0:1]
    shape = (query_count, head_dim)
    lane = lax.broadcasted_iota(jnp.int32, shape, 1)
    own_lane = (lane % query_count == lax.broadcasted_iota(jnp.int32, shape, 0)) & (lane < 3 * query_count)
    levels = jnp.sum(jnp.where(own_lane[None], terms, 0.0), axis=2, keepdims=True)
    own_copy.wait()
    own_mix, own_total, own_top = own[0], own[1], own[2]
    joint = jnp.maximum(jnp.max(levels, axis=0), own_top)
    factor = jnp.exp(levels - joint[None])
    own_factor = jnp.exp(own_top - joint)
    norm = jnp.sum(factor, axis=0) + own_total * own_factor
    mixture = jnp.sum(outs * factor, axis=0) + own_mix * own_factor
    out_ref[...] = (mixture / norm).astype(jnp.bfloat16)


def finish_kernel(arrived_ref, own_ref, out_ref, lent_ref, own, own_sem, lent_sem):
    lent_copy = pltpu.make_async_copy(arrived_ref.at[:, pl.ds(0, lent_ref.shape[1])], lent_ref, lent_sem)
    lent_copy.start()
    join(arrived_ref, own_ref, out_ref, own, own_sem)
    lent_copy.wait()


def finish(arrived, own, page_rows):
    insts, head_dim = arrived.shape[0], arrived.shape[2]
    attended = jax.ShapeDtypeStruct(own.shape[1:], jnp.bfloat16)
    scratch = [pltpu.VMEM(own.shape, own.dtype), pltpu.SemaphoreType.DMA]
    in_place = pl.BlockSpec(memory_space=pl.ANY)
    if page_rows:
        attended = (attended, pltpu.HBM((insts, page_rows, head_dim), arrived.dtype))
        scratch.append(pltpu.SemaphoreType.DMA)
    return pl.pallas_call(
        finish_kernel if page_rows else join,
        out_shape=attended,
        in_specs=[pl.BlockSpec(memory_space=pltpu.VMEM), in_place],
        out_specs=(pl.BlockSpec(memory_space=pltpu.VMEM), in_place)
        if page_rows
        else pl.BlockSpec(memory_space=pltpu.VMEM),
        scratch_shapes=scratch,
        compiler_params=pltpu.CompilerParams(vmem_limit_bytes=8 * MIB),
        name="finish" if page_rows else "join",
    )(in_vmem(arrived), in_hbm(own))


def shards(pool, sectioning, spill_to, tables, lengths, queries, new_kv):
    insts = lax.axis_size("inst")
    resident_slots, half_len, head_dim = pool.shape[0], pool.shape[3], pool.shape[4]
    sectioned = sectioning.shape[0]
    steps = queries.shape[1]
    query_count = steps * queries.shape[2]
    score_scale = head_dim ** (-0.5)
    query_rows = queries.reshape(query_count, head_dim)

    section_pages = sectioning.reshape(sectioned, 2 * half_len, head_dim)
    page_rows = CAP * 2 * half_len
    near_pool = pool.reshape(resident_slots, 2, half_len, head_dim)
    near_section = sectioning.reshape(sectioned, 2, half_len, head_dim)
    far_pool = lax.ppermute(near_pool, "core", [(0, 1), (1, 0)])
    far_section = lax.ppermute(near_section, "core", [(0, 1), (1, 0)])
    whole, paged, asking = pack(spill_to, section_pages, query_rows, insts)

    def exchange(outgoing):
        return lax.all_to_all(outgoing, "inst", split_axis=0, concat_axis=0, tiled=True)

    def owners():
        held_here = (tables[:, :, 0] == lax.axis_index("inst"))[:, :, None] & (
            tables[:, :, 1][:, :, None] == jnp.arange(resident_slots, dtype=jnp.int32)
        )
        request_ids = jnp.arange(tables.shape[0], dtype=jnp.int32)
        return jnp.sum(jnp.where(held_here, request_ids[:, None, None], 0), axis=(0, 1))

    def own_part(far_section):
        length = lax.dynamic_index_in_dim(lengths, lax.axis_index("inst"), 0, keepdims=False)
        place = jnp.stack([length, lax.axis_index("core").astype(jnp.int32)])
        fresh = lax.dynamic_slice_in_dim(new_kv[0], lax.axis_index("pair"), 1, 2)[:, :, 0]
        fresh = jnp.pad(jnp.swapaxes(fresh, 0, 1), ((0, 0), (0, query_count - steps), (0, 0)))
        return own_partial(place, query_rows, near_section, far_section, fresh, score_scale)

    def queries_first(whole, paged, asking, far_pool, far_section):
        asked = exchange(asking)
        own = own_part(far_section)
        paged = resident(owners(), asked, near_pool, far_pool, paged, score_scale, query_count)
        return finish(exchange(paged), own, page_rows)

    def pages_first(whole, paged, asking, far_pool, far_section):
        arrived = exchange(whole)
        own = own_part(far_section)
        partials = resident(owners(), arrived, near_pool, far_pool, None, score_scale, query_count)
        lent = lend(arrived, page_rows)
        return finish(exchange(partials), own, 0), lent

    attended, lent = lax.cond(
        lax.axis_index("core") == 0, queries_first, pages_first, whole, paged, asking, far_pool, far_section
    )
    return attended.reshape(queries.shape), lent.reshape(insts * CAP, 1, 2, half_len, head_dim)


def solution(mesh):
    insts, tp = mesh.devices.shape
    paired = Mesh(mesh.devices.reshape(insts, tp // 2, 2), ("inst", "pair", "core"))
    heads = ("pair", "core")
    return jax.shard_map(
        shards,
        mesh=paired,
        in_specs=(
            P("inst", heads),
            P("inst", heads),
            P("inst"),
            P(),
            P(),
            P("inst", None, heads),
            P("inst"),
        ),
        out_specs=(P("inst", None, heads), P("inst", heads)),
        check_vma=False,
    )
```

time: 91.3 us -> 82.7 us (0.906)
  waiting for transfers between devices: 54.8 us -> 45.4 us
    all_to_all x2, waiting for transfers between devices: 53.4 us -> 45.2 us  [exchange(): lax.all_to_all(outgoing, 'inst', split_axis=0, concat_axis=0, tiled=True)]
    cond x0 -> x12, local copies, waits for them, and re-layouts: none -> 1.94 us
    broadcast_in_dim x1 -> x0, local copies, waits for them, and re-layouts: 1.36 us -> none  [shards(): spread = jnp.broadcast_to(query_rows[None], (insts,) + query_rows.shape)]
    ppermute x1, waiting for transfers between devices: 1.39 us -> 0.23 us  [shards(): far_section = lax.ppermute(near_section, 'core', [(0, 1), (1, 0)])]
  transfers between devices with their start and end apart: 4 -> 4, of which waited for: 3 -> 3; matrix products, arithmetic and copies ran while one was open for 3% -> 3% of each run, Pallas kernels for 4% -> 5%
where the time goes in v3:
time: 82.7 us; the launch traced here: 81.2 us
  waiting for transfers between devices  45.4 us (55%)
  starting transfers between devices  21.7 us (26%)
  Pallas kernels  9 us (11%)
  local copies, waits for them, and re-layouts  3.32 us (4%)
  other arithmetic  0.99 us (1%)
    all_to_all x2, waiting for transfers between devices, exchange(): lax.all_to_all(outgoing, 'inst', split_axis=0, concat_axis=0, tiled=True)  45.2 us
    all_to_all x2, starting transfers between devices, exchange(): lax.all_to_all(outgoing, 'inst', split_axis=0, concat_axis=0, tiled=True)  17.4 us
    pallas_call x1, Pallas kernels, resident(): pl.pallas_call(functools.partial(resident_kernel, score_scale, staged), o...  2.73 us
    ppermute x1, starting transfers between devices, shards(): far_section = lax.ppermute(near_section, 'core', [(0, 1), (1, 0)])  2.41 us
    pallas_call x1, Pallas kernels, pack(): pl.pallas_call(pack_kernel, out_shape=(pltpu.HBM((insts, CAP * rows + que...  2.36 us
    pallas_call x1, Pallas kernels, own_partial(): pl.pallas_call(functools.partial(own_kernel, score_scale), out_shape=jax....  1.97 us
    cond x12, local copies, waits for them, and re-layouts  1.94 us
    pallas_call x1, Pallas kernels, finish(): pl.pallas_call(finish_kernel if page_rows else join, out_shape=attended,...  1.94 us
  transfers between devices with their start and end apart: 4, of which 3 were waited for; matrix products, arithmetic and copies ran while one was open for 3% of the time, Pallas kernels for 5%

profile of v3, /device:TPU:56, one launch (start us, length us, event | category | flops | bytes accessed | tf_op | source)
XLA Modules:
  0.0 81.2 jit_solution(2141013556150755914)
XLA Ops:
  0.6 1.9 %collective-permute-start = (bf16[40,2,64,128]{3,2,1,0:T(8,128)(2,1)}, bf16[40,2,64,128]{3,2,1,0:T(8,128)(2,1)S(1)}, u32[]{:S(2)}, u32[]{:S(2)}) collective-permute-start(bf16[40,2,64,128]{3,2,1,0:T(8,128)(2,1)} %bitcast.30), channel_id=1, source_target_pairs={{0,1},{1,0},{2,3},{3,2},{4,5},{5,4},{6,7},{7,6},{8,9},{9,8},{10,11... | collective-permute-start | bytes 3932168 | tf_op jit(solution)/shard_map/ppermute | solution.py:356
  2.6 2.4 %collective-permute-start.1 = (bf16[32,2,64,128]{3,2,1,0:T(8,128)(2,1)}, bf16[32,2,64,128]{3,2,1,0:T(8,128)(2,1)}, u32[]{:S(2)}, u32[]{:S(2)}) collective-permute-start(bf16[32,2,64,128]{3,2,1,0:T(8,128)(2,1)} %bitcast.33), channel_id=1, source_target_pairs={{0,1},{1,0},{2,3},{3,2},{4,5},{5,4},{6,7},{7,6},{8,9},{9,8},{10,11... | collective-permute-start | bytes 3145736 | tf_op jit(solution)/shard_map/ppermute | solution.py:357
  5.0 2.4 %pack.1 = (bf16[32,272,128]{2,1,0:T(8,128)(2,1)}, bf16[32,280,128]{2,1,0:T(8,128)(2,1)}, bf16[32,16,128]{2,1,0:T(8,128)(2,1)}) custom-call(s32[32]{0:T(128)} %spill_ref.1, bf16[32,128,128]{2,1,0:T(8,128)(2,1)} %bitcast.34, bf16[16,128]{1,0:T(8,128)(2,1)} %bitcast.39), custom_call_target="tpu_custom_call" | custom-call | tf_op jit(solution)/shard_map/pack/pallas_call | solution.py:104
  7.4 0.2 collective-permute-done.1
  7.6 0.0 collective-permute-done
  7.6 73.6 %conditional.1 = (bf16[1,4,4,128]{3,2,1,0:T(4,128)(2,1)}, bf16[64,1,2,64,128]{4,3,2,1,0:T(8,128)(2,1)}) conditional(s32[]{:T(128)} %convert_element_type.6, (s32[32,111,2]{1,2,0:T(2,128)}, bf16[32,272,128]{2,1,0:T(8,128)(2,1)}, bf16[40,2,64,128]{3,2,1,0:T(8,128)(2,1)}, bf16[40,2,64,128]{3,2,1,0:T(8,128)(2,1)S(1)}, s32[32]{0:T(128)}, ...), branch_computations={%region_0.2_spmd, %region_2.4_spmd} | conditional | flops 571848 | bytes 18043894 | solution.py:390
  7.6 13.2 %all-to-all-start.2 = ((bf16[32,16,128]{2,1,0:T(8,128)(2,1)}), bf16[32,16,128]{2,1,0:T(8,128)(2,1)S(1)}, u32[]{:S(2)}, u32[]{:S(2)}) async-start(bf16[32,16,128]{2,1,0:T(8,128)(2,1)} %get-tuple-element.52), calls=%async_computation.2 | async-start | bytes 262144 | tf_op jit(solution)/shard_map/cond/branch_1_fun/all_to_all | solution.py:361
  20.8 0.8 copy.24
  21.5 0.3 select_reduce_fusion.1.owner_ref
  21.8 11.7 %all-to-all-done.2.arrived_ref = bf16[32,16,128]{2,1,0:T(8,128)(2,1)S(1)} async-done(((bf16[32,16,128]{2,1,0:T(8,128)(2,1)}), bf16[32,16,128]{2,1,0:T(8,128)(2,1)S(1)}, u32[]{:S(2)}, u32[]{:S(2)}) %all-to-all-start.2) | async-done | bytes 131104 | tf_op jit(solution)/shard_map/cond/branch_1_fun/all_to_all | solution.py:361
  33.5 0.0 copy-start.1
  33.5 1.3 %copy-done.1 = bf16[40,2,64,128]{3,2,1,0:T(8,128)(2,1)S(1)} copy-done((bf16[40,2,64,128]{3,2,1,0:T(8,128)(2,1)S(1)}, bf16[40,2,64,128]{3,2,1,0:T(8,128)(2,1)}, u32[]{:S(2)}) %copy-start.1) | copy-done | bytes 1310744 | tf_op jit(solution)/shard_map/cond
  34.8 2.7 %resident.1 = bf16[32,280,128]{2,1,0:T(8,128)(2,1)} custom-call(s32[40]{0:T(128)S(1)} %select_reduce_fusion.1.owner_ref, bf16[32,16,128]{2,1,0:T(8,128)(2,1)S(1)} %all-to-all-done.2.arrived_ref, bf16[40,2,64,128]{3,2,1,0:T(8,128)(2,1)S(1)} %copy-done.1, bf16[40,2,64,128]{3,2,1,0:T(8,128)(2,1)S(1)} %get-tuple-element.54.far_ref, ...), custom_call_target="tpu_custom_call", output_to_operand_aliasing={{}: (4, {})} | custom-call | tf_op jit(solution)/shard_map/cond/branch_1_fun/resident/pallas_call | solution.py:216
  37.5 0.0 copy-start.6
  37.5 0.0 copy-start.10
  37.5 0.0 copy-start.5
  37.6 0.0 copy-start.8
  37.6 4.2 %all-to-all-start.3 = ((bf16[32,280,128]{2,1,0:T(8,128)(2,1)}), bf16[32,280,128]{2,1,0:T(8,128)(2,1)S(1)}, u32[]{:S(2)}, u32[]{:S(2)}) async-start(bf16[32,280,128]{2,1,0:T(8,128)(2,1)} %resident.1), calls=%async_computation.3 | async-start | bytes 4587520 | tf_op jit(solution)/shard_map/cond/branch_1_fun/all_to_all | solution.py:361
  41.8 0.0 copy-done.6
  41.8 0.0 copy-done.10
  41.8 0.6 dynamic_slice.11
  42.4 0.7 pad_add_fusion.1.place_ref
  43.1 0.0 copy-done.5
  43.1 0.0 copy-done.8
  43.2 2.0 %own_pages.3.own_ref = f32[3,16,128]{2,1,0:T(8,128)S(1)} custom-call(s32[2]{0:T(128)S(1)} %pad_add_fusion.1.place_ref, bf16[16,128]{1,0:T(8,128)(2,1)S(1)} %copy-done.8, bf16[32,2,64,128]{3,2,1,0:T(8,128)(2,1)S(1)} %copy-done.5, bf16[32,2,64,128]{3,2,1,0:T(8,128)(2,1)} %get-tuple-element.59.far_ref, bf16[2,16,128]{2,1,0:T(8,128)(2,1)S(1)} %pad.6.fresh_ref), custom_call_target="tpu_custom_call" | custom-call | tf_op jit(solution)/shard_map/cond/branch_1_fun/own_pages/pallas_call | solution.py:265
  45.1 0.0 copy-start.3
  45.1 0.6 copy-done.3
  45.7 33.5 %all-to-all-done.3.arrived_ref = bf16[32,280,128]{2,1,0:T(8,128)(2,1)S(1)} async-done(((bf16[32,280,128]{2,1,0:T(8,128)(2,1)}), bf16[32,280,128]{2,1,0:T(8,128)(2,1)S(1)}, u32[]{:S(2)}, u32[]{:S(2)}) %all-to-all-start.3) | async-done | bytes 2293792 | tf_op jit(solution)/shard_map/cond/branch_1_fun/all_to_all | solution.py:361
  79.2 1.9 %finish.1 = (bf16[16,128]{1,0:T(8,128)(2,1)}, bf16[32,256,128]{2,1,0:T(8,128)(2,1)}) custom-call(bf16[32,280,128]{2,1,0:T(8,128)(2,1)S(1)} %all-to-all-done.3.arrived_ref, f32[3,16,128]{2,1,0:T(8,128)} %copy-done.3), custom_call_target="tpu_custom_call" | custom-call | tf_op jit(solution)/shard_map/cond/branch_1_fun/finish/pallas_call | solution.py:330
  (5 shorter events, 0.0 us)
Async XLA Ops:
  0.6 7.0 %collective-permute-start = (bf16[40,2,64,128]{3,2,1,0:T(8,128)(2,1)}, bf16[40,2,64,128]{3,2,1,0:T(8,128)(2,1)S(1)}, u32[]{:S(2)}, u32[]{:S(2)}) collective-permute-start(bf16[40,2,64,128]{3,2,1,0:T(8,128)(2,1)} %bitcast.30), channel_id=1, source_target_pairs={{0,1},{1,0},{2,3},{3,2},{4,5},{5,4},{6,7},{7,6},{8,9},{9,8},{10,11... | collective-permute-start | bytes 3932168 | tf_op jit(solution)/shard_map/ppermute | solution.py:356
  2.6 5.0 %collective-permute-start.1 = (bf16[32,2,64,128]{3,2,1,0:T(8,128)(2,1)}, bf16[32,2,64,128]{3,2,1,0:T(8,128)(2,1)}, u32[]{:S(2)}, u32[]{:S(2)}) collective-permute-start(bf16[32,2,64,128]{3,2,1,0:T(8,128)(2,1)} %bitcast.33), channel_id=1, source_target_pairs={{0,1},{1,0},{2,3},{3,2},{4,5},{5,4},{6,7},{7,6},{8,9},{9,8},{10,11... | collective-permute-start | bytes 3145736 | tf_op jit(solution)/shard_map/ppermute | solution.py:357
  7.6 25.9 %all-to-all-start.2 = ((bf16[32,16,128]{2,1,0:T(8,128)(2,1)}), bf16[32,16,128]{2,1,0:T(8,128)(2,1)S(1)}, u32[]{:S(2)}, u32[]{:S(2)}) async-start(bf16[32,16,128]{2,1,0:T(8,128)(2,1)} %get-tuple-element.52), calls=%async_computation.2 | async-start | bytes 262144 | tf_op jit(solution)/shard_map/cond/branch_1_fun/all_to_all | solution.py:361
  33.5 1.3 %copy-start.1 = (bf16[40,2,64,128]{3,2,1,0:T(8,128)(2,1)S(1)}, bf16[40,2,64,128]{3,2,1,0:T(8,128)(2,1)}, u32[]{:S(2)}) copy-start(bf16[40,2,64,128]{3,2,1,0:T(8,128)(2,1)} %get-tuple-element.53.near_ref) | copy-start | bytes 3932164 | tf_op jit(solution)/shard_map/cond
  37.5 4.3 %copy-start.6 = (bf16[1,4,2,8,128]{4,3,2,1,0:T(8,128)(2,1)S(1)}, bf16[1,4,2,8,128]{4,3,2,1,0:T(8,128)(2,1)}, u32[]{:S(2)}) copy-start(bf16[1,4,2,8,128]{4,3,2,1,0:T(8,128)(2,1)} %get-tuple-element.130) | copy-start | bytes 49156 | tf_op jit(solution)/shard_map/cond
  37.5 4.3 %copy-start.10 = (s32[32]{0:T(128)S(1)}, s32[32]{0:T(128)}, u32[]{:S(2)}) copy-start(s32[32]{0:T(128)} %get-tuple-element.56) | copy-start | bytes 388 | tf_op jit(solution)/shard_map/cond
  37.5 5.6 %copy-start.5 = (bf16[32,2,64,128]{3,2,1,0:T(8,128)(2,1)S(1)}, bf16[32,2,64,128]{3,2,1,0:T(8,128)(2,1)}, u32[]{:S(2)}) copy-start(bf16[32,2,64,128]{3,2,1,0:T(8,128)(2,1)} %get-tuple-element.58.near_ref) | copy-start | bytes 3145732 | tf_op jit(solution)/shard_map/cond
  37.6 5.6 %copy-start.8 = (bf16[16,128]{1,0:T(8,128)(2,1)S(1)}, bf16[16,128]{1,0:T(8,128)(2,1)}, u32[]{:S(2)}) copy-start(bf16[16,128]{1,0:T(8,128)(2,1)} %get-tuple-element.57.query_ref) | copy-start | bytes 12292 | tf_op jit(solution)/shard_map/cond
  37.6 41.7 %all-to-all-start.3 = ((bf16[32,280,128]{2,1,0:T(8,128)(2,1)}), bf16[32,280,128]{2,1,0:T(8,128)(2,1)S(1)}, u32[]{:S(2)}, u32[]{:S(2)}) async-start(bf16[32,280,128]{2,1,0:T(8,128)(2,1)} %resident.1), calls=%async_computation.3 | async-start | bytes 4587520 | tf_op jit(solution)/shard_map/cond/branch_1_fun/all_to_all | solution.py:361
  45.1 0.6 copy-start.3

commit v4 on v3

--- a/solution.py
+++ b/solution.py
@@ -126,37 +126,39 @@
 
 
 def resident_kernel(score_scale, staged, owner_ref, arrived_ref, near_ref, far_ref, *others):
-    copies = []
     if staged:
-        *others, near, far, sems = others
-        for index in range(2):
-            for source, target in ((near_ref, near), (far_ref, far)):
-                copies.append(
-                    pltpu.make_async_copy(source.at[:, index], target.at[:, index], sems.at[len(copies)])
-                )
-                copies[-1].start()
-        near_ref, far_ref = near, far
+        *others, asked, near, sems = others
+        query_count = asked.shape[1]
+        first_query = arrived_ref.shape[1] - query_count
+        copies = [
+            pltpu.make_async_copy(arrived_ref.at[:, pl.ds(first_query, query_count)], asked, sems.at[0]),
+            pltpu.make_async_copy(near_ref.at[:, 0], near.at[:, 0], sems.at[1]),
+            pltpu.make_async_copy(near_ref.at[:, 1], near.at[:, 1], sems.at[2]),
+        ]
+        for copy in copies:
+            copy.start()
+        arrived_ref, near_ref = asked, near
     out_ref, partials, score, top, total, mix, part_sem = others[-7:]
     requests, query_count = mix.shape[0], mix.shape[1]
     slots = near_ref.shape[0]
-    first_query = arrived_ref.shape[1] - query_count
     top[...] = jnp.full(top.shape, NEG, jnp.float32)
     total[...] = jnp.zeros_like(total)
     mix[...] = jnp.zeros_like(mix)
 
-    for copy in copies[:2]:
-        copy.wait()
+    if staged:
+        copies[0].wait()
+        copies[1].wait()
     for slot in range(slots):
         owner = owner_ref[slot]
         keys = jnp.concatenate([near_ref[slot, 0], far_ref[slot, 0]], axis=0)
-        found = lax.dot_general(arrived_ref[owner, first_query:], keys, NT, preferred_element_type=jnp.float32) * score_scale
+        found = lax.dot_general(arrived_ref[owner], keys, NT, preferred_element_type=jnp.float32) * score_scale
         score[slot] = found
         top[owner] = jnp.maximum(top[owner], found)
 
     for request in range(requests):
         top[request] = jnp.broadcast_to(jnp.max(top[request], axis=1, keepdims=True), top.shape[1:])
-    for copy in copies[2:]:
-        copy.wait()
+    if staged:
+        copies[2].wait()
     for slot in range(slots):
         owner = owner_ref[slot]
         weights = jnp.exp(score[slot] - top[owner])
@@ -195,8 +197,6 @@
     part_rows = query_count + STAT_ROWS
     out_shape, aliases = (requests, part_rows, head_dim), {}
     staged = outgoing is None
-    operands = [owner_of, in_vmem(arrived)]
-    spaces = [pltpu.SMEM, pltpu.VMEM]
     scratch = [
         pltpu.VMEM((requests, part_rows, head_dim), arrived.dtype),
         pltpu.VMEM((slots, query_count, tokens), jnp.float32),
@@ -206,13 +206,17 @@
         pltpu.SemaphoreType.DMA,
     ]
     if staged:
-        operands += [near, far]
-        spaces += [pl.ANY] * 2
-        scratch += [pltpu.VMEM(near.shape, near.dtype)] * 2 + [pltpu.SemaphoreType.DMA((4,))]
+        operands = [owner_of, arrived, in_hbm(near), in_vmem(far)]
+        spaces = [pltpu.SMEM, pl.ANY, pl.ANY, pltpu.VMEM]
+        scratch += [
+            pltpu.VMEM((requests, query_count, head_dim), arrived.dtype),
+            pltpu.VMEM(near.shape, near.dtype),
+            pltpu.SemaphoreType.DMA((3,)),
+        ]
     else:
         out_shape, aliases = outgoing.shape, {4: 0}
-        operands += [in_vmem(near), in_vmem(far), in_hbm(outgoing)]
-        spaces += [pltpu.VMEM] * 2 + [pl.ANY]
+        operands = [owner_of, in_vmem(arrived), in_vmem(near), in_vmem(far), in_hbm(outgoing)]
+        spaces = [pltpu.SMEM] + [pltpu.VMEM] * 3 + [pl.ANY]
     return pl.pallas_call(
         functools.partial(resident_kernel, score_scale, staged),
         out_shape=pltpu.HBM(out_shape, arrived.dtype),
@@ -272,10 +276,24 @@
     )(place, query_rows, near, far, fresh)
 
 
-def lend_kernel(arrived_ref, lent_ref, sem):
-    lent_copy = pltpu.make_async_copy(arrived_ref.at[:, pl.ds(0, lent_ref.shape[1])], lent_ref, sem)
-    lent_copy.start()
-    lent_copy.wait()
+def lend_kernel(arrived_ref, lent_ref, pages, sems):
+    pieces = sems.shape[0] // 2
+    count = lent_ref.shape[0] // pieces
+    arriving, leaving = [], []
+    for piece in range(pieces):
+        part = pl.ds(piece * count, count)
+        arriving.append(
+            pltpu.make_async_copy(
+                arrived_ref.at[part, pl.ds(0, lent_ref.shape[1])], pages.at[part], sems.at[2 * piece]
+            )
+        )
+        leaving.append(pltpu.make_async_copy(pages.at[part], lent_ref.at[part], sems.at[2 * piece + 1]))
+        arriving[-1].start()
+    for into, out in zip(arriving, leaving, strict=True):
+        into.wait()
+        out.start()
+    for out in leaving:
+        out.wait()
 
 
 def lend(arrived, page_rows):
@@ -285,10 +303,13 @@
         out_shape=pltpu.HBM((insts, page_rows, head_dim), arrived.dtype),
         in_specs=[pl.BlockSpec(memory_space=pl.ANY)],
         out_specs=pl.BlockSpec(memory_space=pl.ANY),
-        scratch_shapes=[pltpu.SemaphoreType.DMA],
-        compiler_params=pltpu.CompilerParams(vmem_limit_bytes=MIB),
+        scratch_shapes=[
+            pltpu.VMEM((insts, page_rows, head_dim), arrived.dtype),
+            pltpu.SemaphoreType.DMA((8,)),
+        ],
+        compiler_params=pltpu.CompilerParams(vmem_limit_bytes=4 * MIB),
         name="lend",
-    )(in_vmem(arrived))
+    )(arrived)
 
 
 def join(arrived_ref, own_ref, out_ref, own, own_sem):

time: 82.7 us -> 81.9 us (level)
  waiting for transfers between devices: 45.4 us -> 43.2 us
  starting transfers between devices: 21.7 us -> 23 us
    all_to_all x2, waiting for transfers between devices: 45.2 us -> 42.9 us  [exchange(): lax.all_to_all(outgoing, 'inst', split_axis=0, concat_axis=0, tiled=True)]
    all_to_all x2, starting transfers between devices: 17.4 us -> 18.7 us  [exchange(): lax.all_to_all(outgoing, 'inst', split_axis=0, concat_axis=0, tiled=True)]
where the time goes in v4:
time: 81.9 us; the launch traced here: 80.3 us
  waiting for transfers between devices  43.2 us (53%)
  starting transfers between devices  23 us (28%)
  Pallas kernels  8.99 us (11%)
  local copies, waits for them, and re-layouts  3.32 us (4%)
  other arithmetic  0.99 us (1%)
    all_to_all x2, waiting for transfers between devices, exchange(): lax.all_to_all(outgoing, 'inst', split_axis=0, concat_axis=0, tiled=True)  42.9 us
    all_to_all x2, starting transfers between devices, exchange(): lax.all_to_all(outgoing, 'inst', split_axis=0, concat_axis=0, tiled=True)  18.7 us
    pallas_call x1, Pallas kernels, resident(): pl.pallas_call(functools.partial(resident_kernel, score_scale, staged), o...  2.74 us
    ppermute x1, starting transfers between devices, shards(): far_section = lax.ppermute(near_section, 'core', [(0, 1), (1, 0)])  2.41 us
    pallas_call x1, Pallas kernels, pack(): pl.pallas_call(pack_kernel, out_shape=(pltpu.HBM((insts, CAP * rows + que...  2.35 us
    pallas_call x1, Pallas kernels, own_partial(): pl.pallas_call(functools.partial(own_kernel, score_scale), out_shape=jax....  1.97 us
    cond x12, local copies, waits for them, and re-layouts  1.95 us
    pallas_call x1, Pallas kernels, finish(): pl.pallas_call(finish_kernel if page_rows else join, out_shape=attended,...  1.94 us
  transfers between devices with their start and end apart: 4, of which 3 were waited for; matrix products, arithmetic and copies ran while one was open for 3% of the time, Pallas kernels for 5%

profile of v4, /device:TPU:56, one launch (start us, length us, event | category | flops | bytes accessed | tf_op | source)
XLA Modules:
  0.0 80.3 jit_solution(12039285302089724014)
XLA Ops:
  0.6 1.9 %collective-permute-start = (bf16[40,2,64,128]{3,2,1,0:T(8,128)(2,1)}, bf16[40,2,64,128]{3,2,1,0:T(8,128)(2,1)S(1)}, u32[]{:S(2)}, u32[]{:S(2)}) collective-permute-start(bf16[40,2,64,128]{3,2,1,0:T(8,128)(2,1)} %bitcast.30), channel_id=1, source_target_pairs={{0,1},{1,0},{2,3},{3,2},{4,5},{5,4},{6,7},{7,6},{8,9},{9,8},{10,11... | collective-permute-start | bytes 3932168 | tf_op jit(solution)/shard_map/ppermute | solution.py:377
  2.6 2.4 %collective-permute-start.1 = (bf16[32,2,64,128]{3,2,1,0:T(8,128)(2,1)}, bf16[32,2,64,128]{3,2,1,0:T(8,128)(2,1)}, u32[]{:S(2)}, u32[]{:S(2)}) collective-permute-start(bf16[32,2,64,128]{3,2,1,0:T(8,128)(2,1)} %bitcast.33), channel_id=1, source_target_pairs={{0,1},{1,0},{2,3},{3,2},{4,5},{5,4},{6,7},{7,6},{8,9},{9,8},{10,11... | collective-permute-start | bytes 3145736 | tf_op jit(solution)/shard_map/ppermute | solution.py:378
  5.0 2.3 %pack.1 = (bf16[32,272,128]{2,1,0:T(8,128)(2,1)}, bf16[32,280,128]{2,1,0:T(8,128)(2,1)}, bf16[32,16,128]{2,1,0:T(8,128)(2,1)}) custom-call(s32[32]{0:T(128)} %spill_ref.1, bf16[32,128,128]{2,1,0:T(8,128)(2,1)} %bitcast.34, bf16[16,128]{1,0:T(8,128)(2,1)} %bitcast.39), custom_call_target="tpu_custom_call" | custom-call | tf_op jit(solution)/shard_map/pack/pallas_call | solution.py:104
  7.3 0.2 collective-permute-done.1
  7.6 0.0 collective-permute-done
  7.6 72.7 %conditional.1 = (bf16[1,4,4,128]{3,2,1,0:T(4,128)(2,1)}, bf16[64,1,2,64,128]{4,3,2,1,0:T(8,128)(2,1)}) conditional(s32[]{:T(128)} %convert_element_type.6, (s32[32,111,2]{1,2,0:T(2,128)}, bf16[32,272,128]{2,1,0:T(8,128)(2,1)}, bf16[40,2,64,128]{3,2,1,0:T(8,128)(2,1)}, bf16[40,2,64,128]{3,2,1,0:T(8,128)(2,1)S(1)}, s32[32]{0:T(128)}, ...), branch_computations={%region_0.2_spmd, %region_2.4_spmd} | conditional | flops 571848 | bytes 17060886 | solution.py:411
  7.6 13.2 %all-to-all-start.2 = ((bf16[32,16,128]{2,1,0:T(8,128)(2,1)}), bf16[32,16,128]{2,1,0:T(8,128)(2,1)S(1)}, u32[]{:S(2)}, u32[]{:S(2)}) async-start(bf16[32,16,128]{2,1,0:T(8,128)(2,1)} %get-tuple-element.52), calls=%async_computation.2 | async-start | bytes 262144 | tf_op jit(solution)/shard_map/cond/branch_1_fun/all_to_all | solution.py:382
  20.8 0.8 copy.24
  21.6 0.3 select_reduce_fusion.1.owner_ref
  21.8 10.9 %all-to-all-done.2.arrived_ref = bf16[32,16,128]{2,1,0:T(8,128)(2,1)S(1)} async-done(((bf16[32,16,128]{2,1,0:T(8,128)(2,1)}), bf16[32,16,128]{2,1,0:T(8,128)(2,1)S(1)}, u32[]{:S(2)}, u32[]{:S(2)}) %all-to-all-start.2) | async-done | bytes 131104 | tf_op jit(solution)/shard_map/cond/branch_1_fun/all_to_all | solution.py:382
  32.7 0.0 copy-start
  32.7 1.3 %copy-done = bf16[40,2,64,128]{3,2,1,0:T(8,128)(2,1)S(1)} copy-done((bf16[40,2,64,128]{3,2,1,0:T(8,128)(2,1)S(1)}, bf16[40,2,64,128]{3,2,1,0:T(8,128)(2,1)}, u32[]{:S(2)}) %copy-start) | copy-done | bytes 1310744 | tf_op jit(solution)/shard_map/cond
  34.0 2.7 %resident.1 = bf16[32,280,128]{2,1,0:T(8,128)(2,1)} custom-call(s32[40]{0:T(128)S(1)} %select_reduce_fusion.1.owner_ref, bf16[32,16,128]{2,1,0:T(8,128)(2,1)S(1)} %all-to-all-done.2.arrived_ref, bf16[40,2,64,128]{3,2,1,0:T(8,128)(2,1)S(1)} %copy-done, bf16[40,2,64,128]{3,2,1,0:T(8,128)(2,1)S(1)} %get-tuple-element.54.far_ref, ...), custom_call_target="tpu_custom_call", output_to_operand_aliasing={{}: (4, {})} | custom-call | tf_op jit(solution)/shard_map/cond/branch_1_fun/resident/pallas_call | solution.py:220
  36.8 0.0 copy-start.4
  36.8 0.0 copy-start.8
  36.8 0.0 copy-start.3
  36.8 0.0 copy-start.6
  36.8 5.5 %all-to-all-start.3 = ((bf16[32,280,128]{2,1,0:T(8,128)(2,1)}), bf16[32,280,128]{2,1,0:T(8,128)(2,1)S(1)}, u32[]{:S(2)}, u32[]{:S(2)}) async-start(bf16[32,280,128]{2,1,0:T(8,128)(2,1)} %resident.1), calls=%async_computation.3 | async-start | bytes 4587520 | tf_op jit(solution)/shard_map/cond/branch_1_fun/all_to_all | solution.py:382
  42.3 0.0 copy-done.4
  42.4 0.0 copy-done.8
  42.4 0.6 dynamic_slice.11
  43.0 0.7 pad_add_fusion.1.place_ref
  43.7 0.0 copy-done.3
  43.7 0.0 copy-done.6
  43.7 2.0 %own_pages.3.own_ref = f32[3,16,128]{2,1,0:T(8,128)S(1)} custom-call(s32[2]{0:T(128)S(1)} %pad_add_fusion.1.place_ref, bf16[16,128]{1,0:T(8,128)(2,1)S(1)} %copy-done.6, bf16[32,2,64,128]{3,2,1,0:T(8,128)(2,1)S(1)} %copy-done.3, bf16[32,2,64,128]{3,2,1,0:T(8,128)(2,1)} %get-tuple-element.59.far_ref, bf16[2,16,128]{2,1,0:T(8,128)(2,1)S(1)} %pad.6.fresh_ref), custom_call_target="tpu_custom_call" | custom-call | tf_op jit(solution)/shard_map/cond/branch_1_fun/own_pages/pallas_call | solution.py:269
  45.7 0.0 copy-start.1
  45.7 0.6 copy-done.1
  46.3 32.0 %all-to-all-done.3.arrived_ref = bf16[32,280,128]{2,1,0:T(8,128)(2,1)S(1)} async-done(((bf16[32,280,128]{2,1,0:T(8,128)(2,1)}), bf16[32,280,128]{2,1,0:T(8,128)(2,1)S(1)}, u32[]{:S(2)}, u32[]{:S(2)}) %all-to-all-start.3) | async-done | bytes 2293792 | tf_op jit(solution)/shard_map/cond/branch_1_fun/all_to_all | solution.py:382
  78.3 1.9 %finish.1 = (bf16[16,128]{1,0:T(8,128)(2,1)}, bf16[32,256,128]{2,1,0:T(8,128)(2,1)}) custom-call(bf16[32,280,128]{2,1,0:T(8,128)(2,1)S(1)} %all-to-all-done.3.arrived_ref, f32[3,16,128]{2,1,0:T(8,128)} %copy-done.1), custom_call_target="tpu_custom_call" | custom-call | tf_op jit(solution)/shard_map/cond/branch_1_fun/finish/pallas_call | solution.py:351
  (5 shorter events, 0.0 us)
Async XLA Ops:
  0.6 7.0 %collective-permute-start = (bf16[40,2,64,128]{3,2,1,0:T(8,128)(2,1)}, bf16[40,2,64,128]{3,2,1,0:T(8,128)(2,1)S(1)}, u32[]{:S(2)}, u32[]{:S(2)}) collective-permute-start(bf16[40,2,64,128]{3,2,1,0:T(8,128)(2,1)} %bitcast.30), channel_id=1, source_target_pairs={{0,1},{1,0},{2,3},{3,2},{4,5},{5,4},{6,7},{7,6},{8,9},{9,8},{10,11... | collective-permute-start | bytes 3932168 | tf_op jit(solution)/shard_map/ppermute | solution.py:377
  2.6 5.0 %collective-permute-start.1 = (bf16[32,2,64,128]{3,2,1,0:T(8,128)(2,1)}, bf16[32,2,64,128]{3,2,1,0:T(8,128)(2,1)}, u32[]{:S(2)}, u32[]{:S(2)}) collective-permute-start(bf16[32,2,64,128]{3,2,1,0:T(8,128)(2,1)} %bitcast.33), channel_id=1, source_target_pairs={{0,1},{1,0},{2,3},{3,2},{4,5},{5,4},{6,7},{7,6},{8,9},{9,8},{10,11... | collective-permute-start | bytes 3145736 | tf_op jit(solution)/shard_map/ppermute | solution.py:378
  7.6 25.1 %all-to-all-start.2 = ((bf16[32,16,128]{2,1,0:T(8,128)(2,1)}), bf16[32,16,128]{2,1,0:T(8,128)(2,1)S(1)}, u32[]{:S(2)}, u32[]{:S(2)}) async-start(bf16[32,16,128]{2,1,0:T(8,128)(2,1)} %get-tuple-element.52), calls=%async_computation.2 | async-start | bytes 262144 | tf_op jit(solution)/shard_map/cond/branch_1_fun/all_to_all | solution.py:382
  32.7 1.3 %copy-start = (bf16[40,2,64,128]{3,2,1,0:T(8,128)(2,1)S(1)}, bf16[40,2,64,128]{3,2,1,0:T(8,128)(2,1)}, u32[]{:S(2)}) copy-start(bf16[40,2,64,128]{3,2,1,0:T(8,128)(2,1)} %get-tuple-element.53.near_ref) | copy-start | bytes 3932164 | tf_op jit(solution)/shard_map/cond
  36.8 5.6 %copy-start.4 = (bf16[1,4,2,8,128]{4,3,2,1,0:T(8,128)(2,1)S(1)}, bf16[1,4,2,8,128]{4,3,2,1,0:T(8,128)(2,1)}, u32[]{:S(2)}) copy-start(bf16[1,4,2,8,128]{4,3,2,1,0:T(8,128)(2,1)} %get-tuple-element.130) | copy-start | bytes 49156 | tf_op jit(solution)/shard_map/cond
  36.8 5.6 %copy-start.8 = (s32[32]{0:T(128)S(1)}, s32[32]{0:T(128)}, u32[]{:S(2)}) copy-start(s32[32]{0:T(128)} %get-tuple-element.56) | copy-start | bytes 388 | tf_op jit(solution)/shard_map/cond
  36.8 6.9 %copy-start.3 = (bf16[32,2,64,128]{3,2,1,0:T(8,128)(2,1)S(1)}, bf16[32,2,64,128]{3,2,1,0:T(8,128)(2,1)}, u32[]{:S(2)}) copy-start(bf16[32,2,64,128]{3,2,1,0:T(8,128)(2,1)} %get-tuple-element.58.near_ref) | copy-start | bytes 3145732 | tf_op jit(solution)/shard_map/cond
  36.8 6.9 %copy-start.6 = (bf16[16,128]{1,0:T(8,128)(2,1)S(1)}, bf16[16,128]{1,0:T(8,128)(2,1)}, u32[]{:S(2)}) copy-start(bf16[16,128]{1,0:T(8,128)(2,1)} %get-tuple-element.57.query_ref) | copy-start | bytes 12292 | tf_op jit(solution)/shard_map/cond
  36.8 41.5 %all-to-all-start.3 = ((bf16[32,280,128]{2,1,0:T(8,128)(2,1)}), bf16[32,280,128]{2,1,0:T(8,128)(2,1)S(1)}, u32[]{:S(2)}, u32[]{:S(2)}) async-start(bf16[32,280,128]{2,1,0:T(8,128)(2,1)} %resident.1), calls=%async_computation.3 | async-start | bytes 4587520 | tf_op jit(solution)/shard_map/cond/branch_1_fun/all_to_all | solution.py:382
  45.7 0.6 copy-start.1

commit v5 on v4

--- a/solution.py
+++ b/solution.py
@@ -11,7 +11,7 @@
 CAP = 2
 NEG = -1e30
 NEW = 4
-STAT_ROWS = 8
+STAT_ROWS = 16
 MIB = 1024 * 1024
 NT = (((1,), (1,)), ((), ()))
 

time: 81.9 us -> 83.2 us (1.016)
  waiting for transfers between devices: 43.2 us -> 44.5 us
    all_to_all x2, waiting for transfers between devices: 42.9 us -> 44.2 us  [exchange(): lax.all_to_all(outgoing, 'inst', split_axis=0, concat_axis=0, tiled=True)]
where the time goes in v5:
time: 83.2 us; the launch traced here: 81.6 us
  waiting for transfers between devices  44.5 us (53%)
  starting transfers between devices  23 us (28%)
  Pallas kernels  9.02 us (11%)
  local copies, waits for them, and re-layouts  3.33 us (4%)
  other arithmetic  0.99 us (1%)
    all_to_all x2, waiting for transfers between devices, exchange(): lax.all_to_all(outgoing, 'inst', split_axis=0, concat_axis=0, tiled=True)  44.2 us
    all_to_all x2, starting transfers between devices, exchange(): lax.all_to_all(outgoing, 'inst', split_axis=0, concat_axis=0, tiled=True)  18.7 us
    pallas_call x1, Pallas kernels, resident(): pl.pallas_call(functools.partial(resident_kernel, score_scale, staged), o...  2.77 us
    ppermute x1, starting transfers between devices, shards(): far_section = lax.ppermute(near_section, 'core', [(0, 1), (1, 0)])  2.41 us
    pallas_call x1, Pallas kernels, pack(): pl.pallas_call(pack_kernel, out_shape=(pltpu.HBM((insts, CAP * rows + que...  2.34 us
    pallas_call x1, Pallas kernels, own_partial(): pl.pallas_call(functools.partial(own_kernel, score_scale), out_shape=jax....  1.97 us
    cond x12, local copies, waits for them, and re-layouts  1.95 us
    pallas_call x1, Pallas kernels, finish(): pl.pallas_call(finish_kernel if page_rows else join, out_shape=attended,...  1.94 us
  transfers between devices with their start and end apart: 4, of which 3 were waited for; matrix products, arithmetic and copies ran while one was open for 3% of the time, Pallas kernels for 5%

profile of v5, /device:TPU:56, one launch (start us, length us, event | category | flops | bytes accessed | tf_op | source)
XLA Modules:
  0.0 81.6 jit_solution(4587678636889108824)
XLA Ops:
  0.6 1.9 %collective-permute-start = (bf16[40,2,64,128]{3,2,1,0:T(8,128)(2,1)}, bf16[40,2,64,128]{3,2,1,0:T(8,128)(2,1)S(1)}, u32[]{:S(2)}, u32[]{:S(2)}) collective-permute-start(bf16[40,2,64,128]{3,2,1,0:T(8,128)(2,1)} %bitcast.30), channel_id=1, source_target_pairs={{0,1},{1,0},{2,3},{3,2},{4,5},{5,4},{6,7},{7,6},{8,9},{9,8},{10,11... | collective-permute-start | bytes 3932168 | tf_op jit(solution)/shard_map/ppermute | solution.py:377
  2.6 2.4 %collective-permute-start.1 = (bf16[32,2,64,128]{3,2,1,0:T(8,128)(2,1)}, bf16[32,2,64,128]{3,2,1,0:T(8,128)(2,1)}, u32[]{:S(2)}, u32[]{:S(2)}) collective-permute-start(bf16[32,2,64,128]{3,2,1,0:T(8,128)(2,1)} %bitcast.33), channel_id=1, source_target_pairs={{0,1},{1,0},{2,3},{3,2},{4,5},{5,4},{6,7},{7,6},{8,9},{9,8},{10,11... | collective-permute-start | bytes 3145736 | tf_op jit(solution)/shard_map/ppermute | solution.py:378
  5.0 2.3 %pack.1 = (bf16[32,272,128]{2,1,0:T(8,128)(2,1)}, bf16[32,288,128]{2,1,0:T(8,128)(2,1)}, bf16[32,16,128]{2,1,0:T(8,128)(2,1)}) custom-call(s32[32]{0:T(128)} %spill_ref.1, bf16[32,128,128]{2,1,0:T(8,128)(2,1)} %bitcast.34, bf16[16,128]{1,0:T(8,128)(2,1)} %bitcast.39), custom_call_target="tpu_custom_call" | custom-call | tf_op jit(solution)/shard_map/pack/pallas_call | solution.py:104
  7.3 0.3 collective-permute-done.1
  7.6 0.0 collective-permute-done
  7.6 74.0 %conditional.1 = (bf16[1,4,4,128]{3,2,1,0:T(4,128)(2,1)}, bf16[64,1,2,64,128]{4,3,2,1,0:T(8,128)(2,1)}) conditional(s32[]{:T(128)} %convert_element_type.6, (s32[32,111,2]{1,2,0:T(2,128)}, bf16[32,272,128]{2,1,0:T(8,128)(2,1)}, bf16[40,2,64,128]{3,2,1,0:T(8,128)(2,1)}, bf16[40,2,64,128]{3,2,1,0:T(8,128)(2,1)S(1)}, s32[32]{0:T(128)}, ...), branch_computations={%region_0.2_spmd, %region_2.4_spmd} | conditional | flops 571848 | bytes 17257494 | solution.py:411
  7.6 13.2 %all-to-all-start.2 = ((bf16[32,16,128]{2,1,0:T(8,128)(2,1)}), bf16[32,16,128]{2,1,0:T(8,128)(2,1)S(1)}, u32[]{:S(2)}, u32[]{:S(2)}) async-start(bf16[32,16,128]{2,1,0:T(8,128)(2,1)} %get-tuple-element.52), calls=%async_computation.2 | async-start | bytes 262144 | tf_op jit(solution)/shard_map/cond/branch_1_fun/all_to_all | solution.py:382
  20.8 0.8 copy.24
  21.6 0.3 select_reduce_fusion.1.owner_ref
  21.8 10.9 %all-to-all-done.2.arrived_ref = bf16[32,16,128]{2,1,0:T(8,128)(2,1)S(1)} async-done(((bf16[32,16,128]{2,1,0:T(8,128)(2,1)}), bf16[32,16,128]{2,1,0:T(8,128)(2,1)S(1)}, u32[]{:S(2)}, u32[]{:S(2)}) %all-to-all-start.2) | async-done | bytes 131104 | tf_op jit(solution)/shard_map/cond/branch_1_fun/all_to_all | solution.py:382
  32.7 0.0 copy-start
  32.7 1.3 %copy-done = bf16[40,2,64,128]{3,2,1,0:T(8,128)(2,1)S(1)} copy-done((bf16[40,2,64,128]{3,2,1,0:T(8,128)(2,1)S(1)}, bf16[40,2,64,128]{3,2,1,0:T(8,128)(2,1)}, u32[]{:S(2)}) %copy-start) | copy-done | bytes 1310744 | tf_op jit(solution)/shard_map/cond
  34.0 2.8 %resident.1 = bf16[32,288,128]{2,1,0:T(8,128)(2,1)} custom-call(s32[40]{0:T(128)S(1)} %select_reduce_fusion.1.owner_ref, bf16[32,16,128]{2,1,0:T(8,128)(2,1)S(1)} %all-to-all-done.2.arrived_ref, bf16[40,2,64,128]{3,2,1,0:T(8,128)(2,1)S(1)} %copy-done, bf16[40,2,64,128]{3,2,1,0:T(8,128)(2,1)S(1)} %get-tuple-element.54.far_ref, ...), custom_call_target="tpu_custom_call", output_to_operand_aliasing={{}: (4, {})} | custom-call | tf_op jit(solution)/shard_map/cond/branch_1_fun/resident/pallas_call | solution.py:220
  36.8 0.0 copy-start.4
  36.8 0.0 copy-start.8
  36.8 0.0 copy-start.3
  36.8 0.0 copy-start.6
  36.9 5.5 %all-to-all-start.3 = ((bf16[32,288,128]{2,1,0:T(8,128)(2,1)}), bf16[32,288,128]{2,1,0:T(8,128)(2,1)S(1)}, u32[]{:S(2)}, u32[]{:S(2)}) async-start(bf16[32,288,128]{2,1,0:T(8,128)(2,1)} %resident.1), calls=%async_computation.3 | async-start | bytes 4718592 | tf_op jit(solution)/shard_map/cond/branch_1_fun/all_to_all | solution.py:382
  42.4 0.0 copy-done.4
  42.4 0.0 copy-done.8
  42.4 0.6 dynamic_slice.11
  43.0 0.7 pad_add_fusion.1.place_ref
  43.7 0.0 copy-done.3
  43.7 0.0 copy-done.6
  43.7 2.0 %own_pages.3.own_ref = f32[3,16,128]{2,1,0:T(8,128)S(1)} custom-call(s32[2]{0:T(128)S(1)} %pad_add_fusion.1.place_ref, bf16[16,128]{1,0:T(8,128)(2,1)S(1)} %copy-done.6, bf16[32,2,64,128]{3,2,1,0:T(8,128)(2,1)S(1)} %copy-done.3, bf16[32,2,64,128]{3,2,1,0:T(8,128)(2,1)} %get-tuple-element.59.far_ref, bf16[2,16,128]{2,1,0:T(8,128)(2,1)S(1)} %pad.6.fresh_ref), custom_call_target="tpu_custom_call" | custom-call | tf_op jit(solution)/shard_map/cond/branch_1_fun/own_pages/pallas_call | solution.py:269
  45.7 0.0 copy-start.1
  45.7 0.6 copy-done.1
  46.3 33.3 %all-to-all-done.3.arrived_ref = bf16[32,288,128]{2,1,0:T(8,128)(2,1)S(1)} async-done(((bf16[32,288,128]{2,1,0:T(8,128)(2,1)}), bf16[32,288,128]{2,1,0:T(8,128)(2,1)S(1)}, u32[]{:S(2)}, u32[]{:S(2)}) %all-to-all-start.3) | async-done | bytes 2359328 | tf_op jit(solution)/shard_map/cond/branch_1_fun/all_to_all | solution.py:382
  79.7 1.9 %finish.1 = (bf16[16,128]{1,0:T(8,128)(2,1)}, bf16[32,256,128]{2,1,0:T(8,128)(2,1)}) custom-call(bf16[32,288,128]{2,1,0:T(8,128)(2,1)S(1)} %all-to-all-done.3.arrived_ref, f32[3,16,128]{2,1,0:T(8,128)} %copy-done.1), custom_call_target="tpu_custom_call" | custom-call | tf_op jit(solution)/shard_map/cond/branch_1_fun/finish/pallas_call | solution.py:351
  (5 shorter events, 0.0 us)
Async XLA Ops:
  0.6 7.0 %collective-permute-start = (bf16[40,2,64,128]{3,2,1,0:T(8,128)(2,1)}, bf16[40,2,64,128]{3,2,1,0:T(8,128)(2,1)S(1)}, u32[]{:S(2)}, u32[]{:S(2)}) collective-permute-start(bf16[40,2,64,128]{3,2,1,0:T(8,128)(2,1)} %bitcast.30), channel_id=1, source_target_pairs={{0,1},{1,0},{2,3},{3,2},{4,5},{5,4},{6,7},{7,6},{8,9},{9,8},{10,11... | collective-permute-start | bytes 3932168 | tf_op jit(solution)/shard_map/ppermute | solution.py:377
  2.6 5.0 %collective-permute-start.1 = (bf16[32,2,64,128]{3,2,1,0:T(8,128)(2,1)}, bf16[32,2,64,128]{3,2,1,0:T(8,128)(2,1)}, u32[]{:S(2)}, u32[]{:S(2)}) collective-permute-start(bf16[32,2,64,128]{3,2,1,0:T(8,128)(2,1)} %bitcast.33), channel_id=1, source_target_pairs={{0,1},{1,0},{2,3},{3,2},{4,5},{5,4},{6,7},{7,6},{8,9},{9,8},{10,11... | collective-permute-start | bytes 3145736 | tf_op jit(solution)/shard_map/ppermute | solution.py:378
  7.6 25.1 %all-to-all-start.2 = ((bf16[32,16,128]{2,1,0:T(8,128)(2,1)}), bf16[32,16,128]{2,1,0:T(8,128)(2,1)S(1)}, u32[]{:S(2)}, u32[]{:S(2)}) async-start(bf16[32,16,128]{2,1,0:T(8,128)(2,1)} %get-tuple-element.52), calls=%async_computation.2 | async-start | bytes 262144 | tf_op jit(solution)/shard_map/cond/branch_1_fun/all_to_all | solution.py:382
  32.7 1.3 %copy-start = (bf16[40,2,64,128]{3,2,1,0:T(8,128)(2,1)S(1)}, bf16[40,2,64,128]{3,2,1,0:T(8,128)(2,1)}, u32[]{:S(2)}) copy-start(bf16[40,2,64,128]{3,2,1,0:T(8,128)(2,1)} %get-tuple-element.53.near_ref) | copy-start | bytes 3932164 | tf_op jit(solution)/shard_map/cond
  36.8 5.6 %copy-start.4 = (bf16[1,4,2,8,128]{4,3,2,1,0:T(8,128)(2,1)S(1)}, bf16[1,4,2,8,128]{4,3,2,1,0:T(8,128)(2,1)}, u32[]{:S(2)}) copy-start(bf16[1,4,2,8,128]{4,3,2,1,0:T(8,128)(2,1)} %get-tuple-element.130) | copy-start | bytes 49156 | tf_op jit(solution)/shard_map/cond
  36.8 5.6 %copy-start.8 = (s32[32]{0:T(128)S(1)}, s32[32]{0:T(128)}, u32[]{:S(2)}) copy-start(s32[32]{0:T(128)} %get-tuple-element.56) | copy-start | bytes 388 | tf_op jit(solution)/shard_map/cond
  36.8 6.9 %copy-start.3 = (bf16[32,2,64,128]{3,2,1,0:T(8,128)(2,1)S(1)}, bf16[32,2,64,128]{3,2,1,0:T(8,128)(2,1)}, u32[]{:S(2)}) copy-start(bf16[32,2,64,128]{3,2,1,0:T(8,128)(2,1)} %get-tuple-element.58.near_ref) | copy-start | bytes 3145732 | tf_op jit(solution)/shard_map/cond
  36.8 6.9 %copy-start.6 = (bf16[16,128]{1,0:T(8,128)(2,1)S(1)}, bf16[16,128]{1,0:T(8,128)(2,1)}, u32[]{:S(2)}) copy-start(bf16[16,128]{1,0:T(8,128)(2,1)} %get-tuple-element.57.query_ref) | copy-start | bytes 12292 | tf_op jit(solution)/shard_map/cond
  36.9 42.8 %all-to-all-start.3 = ((bf16[32,288,128]{2,1,0:T(8,128)(2,1)}), bf16[32,288,128]{2,1,0:T(8,128)(2,1)S(1)}, u32[]{:S(2)}, u32[]{:S(2)}) async-start(bf16[32,288,128]{2,1,0:T(8,128)(2,1)} %resident.1), calls=%async_computation.3 | async-start | bytes 4718592 | tf_op jit(solution)/shard_map/cond/branch_1_fun/all_to_all | solution.py:382
  45.7 0.6 copy-start.1

commit v6 on v5

--- a/solution.py
+++ b/solution.py
@@ -128,16 +128,18 @@
 def resident_kernel(score_scale, staged, owner_ref, arrived_ref, near_ref, far_ref, *others):
     if staged:
         *others, asked, near, sems = others
-        query_count = asked.shape[1]
-        first_query = arrived_ref.shape[1] - query_count
-        copies = [
-            pltpu.make_async_copy(arrived_ref.at[:, pl.ds(first_query, query_count)], asked, sems.at[0]),
-            pltpu.make_async_copy(near_ref.at[:, 0], near.at[:, 0], sems.at[1]),
-            pltpu.make_async_copy(near_ref.at[:, 1], near.at[:, 1], sems.at[2]),
-        ]
-        for copy in copies:
-            copy.start()
-        arrived_ref, near_ref = asked, near
+        first_query = arrived_ref.shape[1] - asked.shape[1]
+        asked_copy = pltpu.make_async_copy(
+            arrived_ref.at[:, pl.ds(first_query, asked.shape[1])], asked, sems.at[2]
+        )
+        asked_copy.start()
+    else:
+        *others, near, sems = others
+    key_copy = pltpu.make_async_copy(near_ref.at[:, 0], near.at[:, 0], sems.at[0])
+    value_copy = pltpu.make_async_copy(near_ref.at[:, 1], near.at[:, 1], sems.at[1])
+    key_copy.start()
+    value_copy.start()
+    near_ref = near
     out_ref, partials, score, top, total, mix, part_sem = others[-7:]
     requests, query_count = mix.shape[0], mix.shape[1]
     slots = near_ref.shape[0]
@@ -145,20 +147,25 @@
     total[...] = jnp.zeros_like(total)
     mix[...] = jnp.zeros_like(mix)
 
+    half_len = near_ref.shape[2]
     if staged:
-        copies[0].wait()
-        copies[1].wait()
+        asked_copy.wait()
+        arrived_ref = asked
+
+    def scores(slot, keys):
+        asked_rows = arrived_ref[owner_ref[slot]]
+        return lax.dot_general(asked_rows, keys, NT, preferred_element_type=jnp.float32) * score_scale
+
+    for slot in range(slots):
+        score[slot, :, half_len:] = scores(slot, far_ref[slot, 0])
+    key_copy.wait()
     for slot in range(slots):
         owner = owner_ref[slot]
-        keys = jnp.concatenate([near_ref[slot, 0], far_ref[slot, 0]], axis=0)
-        found = lax.dot_general(arrived_ref[owner], keys, NT, preferred_element_type=jnp.float32) * score_scale
-        score[slot] = found
-        top[owner] = jnp.maximum(top[owner], found)
-
+        score[slot, :, :half_len] = scores(slot, near_ref[slot, 0])
+        top[owner] = jnp.maximum(top[owner], score[slot])
     for request in range(requests):
         top[request] = jnp.broadcast_to(jnp.max(top[request], axis=1, keepdims=True), top.shape[1:])
-    if staged:
-        copies[2].wait()
+    value_copy.wait()
     for slot in range(slots):
         owner = owner_ref[slot]
         weights = jnp.exp(score[slot] - top[owner])
@@ -208,15 +215,12 @@
     if staged:
         operands = [owner_of, arrived, in_hbm(near), in_vmem(far)]
         spaces = [pltpu.SMEM, pl.ANY, pl.ANY, pltpu.VMEM]
-        scratch += [
-            pltpu.VMEM((requests, query_count, head_dim), arrived.dtype),
-            pltpu.VMEM(near.shape, near.dtype),
-            pltpu.SemaphoreType.DMA((3,)),
-        ]
+        scratch.append(pltpu.VMEM((requests, query_count, head_dim), arrived.dtype))
     else:
         out_shape, aliases = outgoing.shape, {4: 0}
-        operands = [owner_of, in_vmem(arrived), in_vmem(near), in_vmem(far), in_hbm(outgoing)]
-        spaces = [pltpu.SMEM] + [pltpu.VMEM] * 3 + [pl.ANY]
+        operands = [owner_of, in_vmem(arrived), in_hbm(near), in_vmem(far), in_hbm(outgoing)]
+        spaces = [pltpu.SMEM, pltpu.VMEM, pl.ANY, pltpu.VMEM, pl.ANY]
+    scratch += [pltpu.VMEM(near.shape, near.dtype), pltpu.SemaphoreType.DMA((3,))]
     return pl.pallas_call(
         functools.partial(resident_kernel, score_scale, staged),
         out_shape=pltpu.HBM(out_shape, arrived.dtype),

time: 83.2 us -> 83.1 us (level)
  local copies, waits for them, and re-layouts: 3.33 us -> 2.01 us
  Pallas kernels: 9.02 us -> 10.1 us
    cond x12 -> x10, local copies, waits for them, and re-layouts: 1.95 us -> 0.64 us
    pallas_call x1, Pallas kernels: 2.77 us -> 3.83 us  [resident(): pl.pallas_call(functools.partial(resident_kernel, score_scale, staged), o...]
where the time goes in v6:
time: 83.1 us; the launch traced here: 81.8 us
  waiting for transfers between devices  44.9 us (54%)
  starting transfers between devices  23 us (28%)
  Pallas kernels  10.1 us (12%)
  local copies, waits for them, and re-layouts  2.01 us (2%)
  other arithmetic  0.99 us (1%)
    all_to_all x2, waiting for transfers between devices, exchange(): lax.all_to_all(outgoing, 'inst', split_axis=0, concat_axis=0, tiled=True)  44.7 us
    all_to_all x2, starting transfers between devices, exchange(): lax.all_to_all(outgoing, 'inst', split_axis=0, concat_axis=0, tiled=True)  18.7 us
    pallas_call x1, Pallas kernels, resident(): pl.pallas_call(functools.partial(resident_kernel, score_scale, staged), o...  3.83 us
    ppermute x1, starting transfers between devices, shards(): far_section = lax.ppermute(near_section, 'core', [(0, 1), (1, 0)])  2.41 us
    pallas_call x1, Pallas kernels, pack(): pl.pallas_call(pack_kernel, out_shape=(pltpu.HBM((insts, CAP * rows + que...  2.36 us
    pallas_call x1, Pallas kernels, own_partial(): pl.pallas_call(functools.partial(own_kernel, score_scale), out_shape=jax....  1.97 us
    pallas_call x1, Pallas kernels, finish(): pl.pallas_call(finish_kernel if page_rows else join, out_shape=attended,...  1.94 us
    ppermute x1, starting transfers between devices, shards(): far_pool = lax.ppermute(near_pool, 'core', [(0, 1), (1, 0)])  1.92 us
  transfers between devices with their start and end apart: 4, of which 3 were waited for; matrix products, arithmetic and copies ran while one was open for 3% of the time, Pallas kernels for 5%

profile of v6, /device:TPU:56, one launch (start us, length us, event | category | flops | bytes accessed | tf_op | source)
XLA Modules:
  0.0 81.8 jit_solution(16719813510645393663)
XLA Ops:
  0.6 1.9 %collective-permute-start = (bf16[40,2,64,128]{3,2,1,0:T(8,128)(2,1)}, bf16[40,2,64,128]{3,2,1,0:T(8,128)(2,1)S(1)}, u32[]{:S(2)}, u32[]{:S(2)}) collective-permute-start(bf16[40,2,64,128]{3,2,1,0:T(8,128)(2,1)} %bitcast.34), channel_id=1, source_target_pairs={{0,1},{1,0},{2,3},{3,2},{4,5},{5,4},{6,7},{7,6},{8,9},{9,8},{10,11... | collective-permute-start | bytes 3932168 | tf_op jit(solution)/shard_map/ppermute | solution.py:381
  2.6 2.4 %collective-permute-start.1 = (bf16[32,2,64,128]{3,2,1,0:T(8,128)(2,1)}, bf16[32,2,64,128]{3,2,1,0:T(8,128)(2,1)}, u32[]{:S(2)}, u32[]{:S(2)}) collective-permute-start(bf16[32,2,64,128]{3,2,1,0:T(8,128)(2,1)} %bitcast.30), channel_id=1, source_target_pairs={{0,1},{1,0},{2,3},{3,2},{4,5},{5,4},{6,7},{7,6},{8,9},{9,8},{10,11... | collective-permute-start | bytes 3145736 | tf_op jit(solution)/shard_map/ppermute | solution.py:382
  5.0 2.4 %pack.1 = (bf16[32,272,128]{2,1,0:T(8,128)(2,1)}, bf16[32,288,128]{2,1,0:T(8,128)(2,1)}, bf16[32,16,128]{2,1,0:T(8,128)(2,1)}) custom-call(s32[32]{0:T(128)} %spill_ref.1, bf16[32,128,128]{2,1,0:T(8,128)(2,1)} %bitcast.31, bf16[16,128]{1,0:T(8,128)(2,1)} %bitcast.39), custom_call_target="tpu_custom_call" | custom-call | tf_op jit(solution)/shard_map/pack/pallas_call | solution.py:104
  7.3 0.2 collective-permute-done.1
  7.6 0.0 collective-permute-done
  7.6 74.2 %conditional.1 = (bf16[1,4,4,128]{3,2,1,0:T(4,128)(2,1)}, bf16[64,1,2,64,128]{4,3,2,1,0:T(8,128)(2,1)}) conditional(s32[]{:T(128)} %convert_element_type.6, (s32[32,111,2]{1,2,0:T(2,128)}, bf16[32,272,128]{2,1,0:T(8,128)(2,1)}, bf16[40,2,64,128]{3,2,1,0:T(8,128)(2,1)}, bf16[40,2,64,128]{3,2,1,0:T(8,128)(2,1)S(1)}, s32[32]{0:T(128)}, ...), branch_computations={%region_0.2_spmd, %region_2.4_spmd} | conditional | flops 571848 | bytes 12014586 | solution.py:415
  7.6 13.2 %all-to-all-start.2 = ((bf16[32,16,128]{2,1,0:T(8,128)(2,1)}), bf16[32,16,128]{2,1,0:T(8,128)(2,1)S(1)}, u32[]{:S(2)}, u32[]{:S(2)}) async-start(bf16[32,16,128]{2,1,0:T(8,128)(2,1)} %get-tuple-element.52), calls=%async_computation.2 | async-start | bytes 262144 | tf_op jit(solution)/shard_map/cond/branch_1_fun/all_to_all | solution.py:386
  20.8 0.8 copy.24
  21.6 0.3 select_reduce_fusion.1.owner_ref
  21.8 10.9 %all-to-all-done.2.arrived_ref = bf16[32,16,128]{2,1,0:T(8,128)(2,1)S(1)} async-done(((bf16[32,16,128]{2,1,0:T(8,128)(2,1)}), bf16[32,16,128]{2,1,0:T(8,128)(2,1)S(1)}, u32[]{:S(2)}, u32[]{:S(2)}) %all-to-all-start.2) | async-done | bytes 131104 | tf_op jit(solution)/shard_map/cond/branch_1_fun/all_to_all | solution.py:386
  32.7 3.8 %resident.1 = bf16[32,288,128]{2,1,0:T(8,128)(2,1)} custom-call(s32[40]{0:T(128)S(1)} %select_reduce_fusion.1.owner_ref, bf16[32,16,128]{2,1,0:T(8,128)(2,1)S(1)} %all-to-all-done.2.arrived_ref, bf16[40,2,64,128]{3,2,1,0:T(8,128)(2,1)} %get-tuple-element.53.near_ref, ...), custom_call_target="tpu_custom_call", output_to_operand_aliasing={{}: (4, {})} | custom-call | tf_op jit(solution)/shard_map/cond/branch_1_fun/resident/pallas_call | solution.py:224
  36.6 0.0 copy-start.3
  36.6 0.0 copy-start.7
  36.6 0.0 copy-start.2
  36.6 0.0 copy-start.5
  36.6 5.5 %all-to-all-start.3 = ((bf16[32,288,128]{2,1,0:T(8,128)(2,1)}), bf16[32,288,128]{2,1,0:T(8,128)(2,1)S(1)}, u32[]{:S(2)}, u32[]{:S(2)}) async-start(bf16[32,288,128]{2,1,0:T(8,128)(2,1)} %resident.1), calls=%async_computation.3 | async-start | bytes 4718592 | tf_op jit(solution)/shard_map/cond/branch_1_fun/all_to_all | solution.py:386
  42.1 0.0 copy-done.3
  42.1 0.0 copy-done.7
  42.2 0.6 dynamic_slice.11
  42.8 0.7 pad_add_fusion.1.place_ref
  43.5 0.0 copy-done.2
  43.5 0.0 copy-done.5
  43.5 2.0 %own_pages.3.own_ref = f32[3,16,128]{2,1,0:T(8,128)S(1)} custom-call(s32[2]{0:T(128)S(1)} %pad_add_fusion.1.place_ref, bf16[16,128]{1,0:T(8,128)(2,1)S(1)} %copy-done.5, bf16[32,2,64,128]{3,2,1,0:T(8,128)(2,1)S(1)} %copy-done.2, bf16[32,2,64,128]{3,2,1,0:T(8,128)(2,1)} %get-tuple-element.59.far_ref, bf16[2,16,128]{2,1,0:T(8,128)(2,1)S(1)} %pad.6.fresh_ref), custom_call_target="tpu_custom_call" | custom-call | tf_op jit(solution)/shard_map/cond/branch_1_fun/own_pages/pallas_call | solution.py:273
  45.5 0.0 copy-start
  45.5 0.6 copy-done
  46.1 33.8 %all-to-all-done.3.arrived_ref = bf16[32,288,128]{2,1,0:T(8,128)(2,1)S(1)} async-done(((bf16[32,288,128]{2,1,0:T(8,128)(2,1)}), bf16[32,288,128]{2,1,0:T(8,128)(2,1)S(1)}, u32[]{:S(2)}, u32[]{:S(2)}) %all-to-all-start.3) | async-done | bytes 2359328 | tf_op jit(solution)/shard_map/cond/branch_1_fun/all_to_all | solution.py:386
  79.8 1.9 %finish.1 = (bf16[16,128]{1,0:T(8,128)(2,1)}, bf16[32,256,128]{2,1,0:T(8,128)(2,1)}) custom-call(bf16[32,288,128]{2,1,0:T(8,128)(2,1)S(1)} %all-to-all-done.3.arrived_ref, f32[3,16,128]{2,1,0:T(8,128)} %copy-done), custom_call_target="tpu_custom_call" | custom-call | tf_op jit(solution)/shard_map/cond/branch_1_fun/finish/pallas_call | solution.py:355
  (5 shorter events, 0.0 us)
Async XLA Ops:
  0.6 7.0 %collective-permute-start = (bf16[40,2,64,128]{3,2,1,0:T(8,128)(2,1)}, bf16[40,2,64,128]{3,2,1,0:T(8,128)(2,1)S(1)}, u32[]{:S(2)}, u32[]{:S(2)}) collective-permute-start(bf16[40,2,64,128]{3,2,1,0:T(8,128)(2,1)} %bitcast.34), channel_id=1, source_target_pairs={{0,1},{1,0},{2,3},{3,2},{4,5},{5,4},{6,7},{7,6},{8,9},{9,8},{10,11... | collective-permute-start | bytes 3932168 | tf_op jit(solution)/shard_map/ppermute | solution.py:381
  2.6 5.0 %collective-permute-start.1 = (bf16[32,2,64,128]{3,2,1,0:T(8,128)(2,1)}, bf16[32,2,64,128]{3,2,1,0:T(8,128)(2,1)}, u32[]{:S(2)}, u32[]{:S(2)}) collective-permute-start(bf16[32,2,64,128]{3,2,1,0:T(8,128)(2,1)} %bitcast.30), channel_id=1, source_target_pairs={{0,1},{1,0},{2,3},{3,2},{4,5},{5,4},{6,7},{7,6},{8,9},{9,8},{10,11... | collective-permute-start | bytes 3145736 | tf_op jit(solution)/shard_map/ppermute | solution.py:382
  7.6 25.1 %all-to-all-start.2 = ((bf16[32,16,128]{2,1,0:T(8,128)(2,1)}), bf16[32,16,128]{2,1,0:T(8,128)(2,1)S(1)}, u32[]{:S(2)}, u32[]{:S(2)}) async-start(bf16[32,16,128]{2,1,0:T(8,128)(2,1)} %get-tuple-element.52), calls=%async_computation.2 | async-start | bytes 262144 | tf_op jit(solution)/shard_map/cond/branch_1_fun/all_to_all | solution.py:386
  36.6 5.6 %copy-start.3 = (bf16[1,4,2,8,128]{4,3,2,1,0:T(8,128)(2,1)S(1)}, bf16[1,4,2,8,128]{4,3,2,1,0:T(8,128)(2,1)}, u32[]{:S(2)}) copy-start(bf16[1,4,2,8,128]{4,3,2,1,0:T(8,128)(2,1)} %get-tuple-element.130) | copy-start | bytes 49156 | tf_op jit(solution)/shard_map/cond
  36.6 5.6 %copy-start.7 = (s32[32]{0:T(128)S(1)}, s32[32]{0:T(128)}, u32[]{:S(2)}) copy-start(s32[32]{0:T(128)} %get-tuple-element.56) | copy-start | bytes 388 | tf_op jit(solution)/shard_map/cond
  36.6 6.9 %copy-start.2 = (bf16[32,2,64,128]{3,2,1,0:T(8,128)(2,1)S(1)}, bf16[32,2,64,128]{3,2,1,0:T(8,128)(2,1)}, u32[]{:S(2)}) copy-start(bf16[32,2,64,128]{3,2,1,0:T(8,128)(2,1)} %get-tuple-element.58.near_ref) | copy-start | bytes 3145732 | tf_op jit(solution)/shard_map/cond
  36.6 6.9 %copy-start.5 = (bf16[16,128]{1,0:T(8,128)(2,1)S(1)}, bf16[16,128]{1,0:T(8,128)(2,1)}, u32[]{:S(2)}) copy-start(bf16[16,128]{1,0:T(8,128)(2,1)} %get-tuple-element.57.query_ref) | copy-start | bytes 12292 | tf_op jit(solution)/shard_map/cond
  36.6 43.2 %all-to-all-start.3 = ((bf16[32,288,128]{2,1,0:T(8,128)(2,1)}), bf16[32,288,128]{2,1,0:T(8,128)(2,1)S(1)}, u32[]{:S(2)}, u32[]{:S(2)}) async-start(bf16[32,288,128]{2,1,0:T(8,128)(2,1)} %resident.1), calls=%async_computation.3 | async-start | bytes 4718592 | tf_op jit(solution)/shard_map/cond/branch_1_fun/all_to_all | solution.py:386
  45.5 0.6 copy-start

commit v7 on v6

--- a/solution.py
+++ b/solution.py
@@ -34,7 +34,6 @@
     spill,
     place,
     count,
-    pages,
     zeros,
     asked,
     spread,
@@ -44,11 +43,9 @@
     sectioned, rows = section_ref.shape[0], section_ref.shape[1]
     core = lax.axis_index("core")
     spill_copy = pltpu.make_async_copy(spill_ref, spill, sems.at[0])
-    page_copy = pltpu.make_async_copy(section_ref, pages, sems.at[1])
     query_copy = pltpu.make_async_copy(query_ref, asked, sems.at[2])
     spill_copy.start()
     query_copy.start()
-    page_copy.start()
     zeros[...] = jnp.zeros_like(zeros)
     for dest in range(insts):
         count[dest] = 0
@@ -78,11 +75,10 @@
         spread[...] = jnp.broadcast_to(asked[...][None], spread.shape)
         spread_copy = pltpu.make_async_copy(spread, query_rows_ref, sems.at[4])
         spread_copy.start()
-        page_copy.wait()
 
         @pl.loop(0, sectioned)
         def _(row):
-            slot_copy(pages.at[row], spill[row], place[row]).start()
+            slot_copy(section_ref.at[row], spill[row], place[row]).start()
 
         all_slots = out_ref.at[:, pl.ds(0, CAP * rows)]
         pltpu.make_async_copy(all_slots, all_slots, sems.at[3]).wait()
@@ -108,13 +104,12 @@
             pltpu.HBM((insts, CAP * rows + query_count + STAT_ROWS, head_dim), dtype),
             pltpu.HBM((insts, query_count, head_dim), dtype),
         ),
-        in_specs=[pl.BlockSpec(memory_space=pl.ANY)] * 3,
+        in_specs=[pl.BlockSpec(memory_space=space) for space in (pl.ANY, pltpu.VMEM, pl.ANY)],
         out_specs=[pl.BlockSpec(memory_space=pl.ANY)] * 3,
         scratch_shapes=[
             pltpu.SMEM(spill_to.shape, jnp.int32),
             pltpu.SMEM(spill_to.shape, jnp.int32),
             pltpu.SMEM((insts,), jnp.int32),
-            pltpu.VMEM(section_pages.shape, dtype),
             pltpu.VMEM((rows, head_dim), dtype),
             pltpu.VMEM(query_rows.shape, dtype),
             pltpu.VMEM((insts,) + query_rows.shape, dtype),
@@ -122,7 +117,7 @@
         ],
         compiler_params=pltpu.CompilerParams(vmem_limit_bytes=4 * MIB),
         name="pack",
-    )(in_hbm(spill_to), in_hbm(section_pages), in_hbm(query_rows))
+    )(in_hbm(spill_to), in_vmem(section_pages), in_hbm(query_rows))
 
 
 def resident_kernel(score_scale, staged, owner_ref, arrived_ref, near_ref, far_ref, *others):

time: 83.1 us -> 84 us (1.011)
  Pallas kernels: 10.1 us -> 11.7 us
  waiting for transfers between devices: 44.9 us -> 44 us
    pallas_call x1, Pallas kernels: 2.36 us -> 3.57 us  [pack(): pl.pallas_call(pack_kernel, out_shape=(pltpu.HBM((insts, CAP * rows + que...]
  transfers between devices with their start and end apart: 4 -> 4, of which waited for: 3 -> 2; matrix products, arithmetic and copies ran while one was open for 3% -> 3% of each run, Pallas kernels for 5% -> 7%
where the time goes in v7:
time: 84 us; the launch traced here: 82.4 us
  waiting for transfers between devices  44 us (52%)
  starting transfers between devices  23 us (27%)
  Pallas kernels  11.7 us (14%)
  local copies, waits for them, and re-layouts  2 us (2%)
  other arithmetic  0.99 us (1%)
    all_to_all x2, waiting for transfers between devices, exchange(): lax.all_to_all(outgoing, 'inst', split_axis=0, concat_axis=0, tiled=True)  44 us
    all_to_all x2, starting transfers between devices, exchange(): lax.all_to_all(outgoing, 'inst', split_axis=0, concat_axis=0, tiled=True)  18.6 us
    pallas_call x1, Pallas kernels, resident(): pl.pallas_call(functools.partial(resident_kernel, score_scale, staged), o...  3.88 us
    pallas_call x1, Pallas kernels, pack(): pl.pallas_call(pack_kernel, out_shape=(pltpu.HBM((insts, CAP * rows + que...  3.57 us
    ppermute x1, starting transfers between devices, shards(): far_section = lax.ppermute(near_section, 'core', [(0, 1), (1, 0)])  2.41 us
    pallas_call x1, Pallas kernels, own_partial(): pl.pallas_call(functools.partial(own_kernel, score_scale), out_shape=jax....  2.28 us
    pallas_call x1, Pallas kernels, finish(): pl.pallas_call(finish_kernel if page_rows else join, out_shape=attended,...  1.94 us
    ppermute x1, starting transfers between devices, shards(): far_pool = lax.ppermute(near_pool, 'core', [(0, 1), (1, 0)])  1.92 us
  transfers between devices with their start and end apart: 4, of which 2 were waited for; matrix products, arithmetic and copies ran while one was open for 3% of the time, Pallas kernels for 7%

profile of v7, /device:TPU:56, one launch (start us, length us, event | category | flops | bytes accessed | tf_op | source)
XLA Modules:
  0.0 82.4 jit_solution(11442200116243888255)
XLA Ops:
  0.6 1.9 %collective-permute-start = (bf16[40,2,64,128]{3,2,1,0:T(8,128)(2,1)}, bf16[40,2,64,128]{3,2,1,0:T(8,128)(2,1)S(1)}, u32[]{:S(2)}, u32[]{:S(2)}) collective-permute-start(bf16[40,2,64,128]{3,2,1,0:T(8,128)(2,1)} %bitcast.30), channel_id=1, source_target_pairs={{0,1},{1,0},{2,3},{3,2},{4,5},{5,4},{6,7},{7,6},{8,9},{9,8},{10,11... | collective-permute-start | bytes 3932168 | tf_op jit(solution)/shard_map/ppermute | solution.py:376
  2.6 2.4 %collective-permute-start.1 = (bf16[32,2,64,128]{3,2,1,0:T(8,128)(2,1)}, bf16[32,2,64,128]{3,2,1,0:T(8,128)(2,1)}, u32[]{:S(2)}, u32[]{:S(2)}) collective-permute-start(bf16[32,2,64,128]{3,2,1,0:T(8,128)(2,1)} %bitcast.23), channel_id=1, source_target_pairs={{0,1},{1,0},{2,3},{3,2},{4,5},{5,4},{6,7},{7,6},{8,9},{9,8},{10,11... | collective-permute-start | bytes 3145736 | tf_op jit(solution)/shard_map/ppermute | solution.py:377
  5.0 3.6 %pack.1 = (bf16[32,272,128]{2,1,0:T(8,128)(2,1)}, bf16[32,288,128]{2,1,0:T(8,128)(2,1)}, bf16[32,16,128]{2,1,0:T(8,128)(2,1)}) custom-call(s32[32]{0:T(128)} %spill_ref.1, bf16[32,128,128]{2,1,0:T(8,128)(2,1)} %bitcast.20.section_ref, bf16[16,128]{1,0:T(8,128)(2,1)} %bitcast.35), custom_call_target="tpu_custom_call" | custom-call | tf_op jit(solution)/shard_map/pack/pallas_call | solution.py:100
  8.6 0.0 collective-permute-done.1
  8.6 0.0 collective-permute-done
  8.6 73.9 %conditional.1 = (bf16[1,4,4,128]{3,2,1,0:T(4,128)(2,1)}, bf16[64,1,2,64,128]{4,3,2,1,0:T(8,128)(2,1)}) conditional(s32[]{:T(128)} %convert_element_type.6, (s32[32,111,2]{1,2,0:T(2,128)}, bf16[32,272,128]{2,1,0:T(8,128)(2,1)}, bf16[40,2,64,128]{3,2,1,0:T(8,128)(2,1)}, bf16[40,2,64,128]{3,2,1,0:T(8,128)(2,1)S(1)}, s32[32]{0:T(128)}, ...), branch_computations={%region_0.2_spmd, %region_2.4_spmd} | conditional | flops 571848 | bytes 7820254 | solution.py:410
  8.6 13.2 %all-to-all-start.2 = ((bf16[32,16,128]{2,1,0:T(8,128)(2,1)}), bf16[32,16,128]{2,1,0:T(8,128)(2,1)S(1)}, u32[]{:S(2)}, u32[]{:S(2)}) async-start(bf16[32,16,128]{2,1,0:T(8,128)(2,1)} %get-tuple-element.52), calls=%async_computation.2 | async-start | bytes 262144 | tf_op jit(solution)/shard_map/cond/branch_1_fun/all_to_all | solution.py:381
  21.8 0.8 copy.24
  22.6 0.3 select_reduce_fusion.1.owner_ref
  22.8 10.5 %all-to-all-done.2.arrived_ref = bf16[32,16,128]{2,1,0:T(8,128)(2,1)S(1)} async-done(((bf16[32,16,128]{2,1,0:T(8,128)(2,1)}), bf16[32,16,128]{2,1,0:T(8,128)(2,1)S(1)}, u32[]{:S(2)}, u32[]{:S(2)}) %all-to-all-start.2) | async-done | bytes 131104 | tf_op jit(solution)/shard_map/cond/branch_1_fun/all_to_all | solution.py:381
  33.4 3.9 %resident.1 = bf16[32,288,128]{2,1,0:T(8,128)(2,1)} custom-call(s32[40]{0:T(128)S(1)} %select_reduce_fusion.1.owner_ref, bf16[32,16,128]{2,1,0:T(8,128)(2,1)S(1)} %all-to-all-done.2.arrived_ref, bf16[40,2,64,128]{3,2,1,0:T(8,128)(2,1)} %get-tuple-element.53.near_ref, ...), custom_call_target="tpu_custom_call", output_to_operand_aliasing={{}: (4, {})} | custom-call | tf_op jit(solution)/shard_map/cond/branch_1_fun/resident/pallas_call | solution.py:219
  37.3 0.0 copy-start.2
  37.3 0.0 copy-start.6
  37.3 0.0 copy-start.4
  37.3 5.4 %all-to-all-start.3 = ((bf16[32,288,128]{2,1,0:T(8,128)(2,1)}), bf16[32,288,128]{2,1,0:T(8,128)(2,1)S(1)}, u32[]{:S(2)}, u32[]{:S(2)}) async-start(bf16[32,288,128]{2,1,0:T(8,128)(2,1)} %resident.1), calls=%async_computation.3 | async-start | bytes 4718592 | tf_op jit(solution)/shard_map/cond/branch_1_fun/all_to_all | solution.py:381
  42.8 0.0 copy-done.2
  42.8 0.0 copy-done.6
  42.8 0.6 dynamic_slice.11
  43.4 0.7 pad_add_fusion.1.place_ref
  44.1 0.0 copy-done.4
  44.1 2.3 %own_pages.3.own_ref = f32[3,16,128]{2,1,0:T(8,128)S(1)} custom-call(s32[2]{0:T(128)S(1)} %pad_add_fusion.1.place_ref, bf16[16,128]{1,0:T(8,128)(2,1)S(1)} %copy-done.4, bf16[32,2,64,128]{3,2,1,0:T(8,128)(2,1)} %get-tuple-element.58.near_ref, bf16[32,2,64,128]{3,2,1,0:T(8,128)(2,1)} %get-tuple-element.59.far_ref, bf16[2,16,128]{2,1,0:T(8,128)(2,1)S(1)} %pad.6.fresh_ref), custom_call_target="tpu_custom_call" | custom-call | tf_op jit(solution)/shard_map/cond/branch_1_fun/own_pages/pallas_call | solution.py:268
  46.4 0.0 copy-start
  46.4 0.6 copy-done
  47.0 33.5 %all-to-all-done.3.arrived_ref = bf16[32,288,128]{2,1,0:T(8,128)(2,1)S(1)} async-done(((bf16[32,288,128]{2,1,0:T(8,128)(2,1)}), bf16[32,288,128]{2,1,0:T(8,128)(2,1)S(1)}, u32[]{:S(2)}, u32[]{:S(2)}) %all-to-all-start.3) | async-done | bytes 2359328 | tf_op jit(solution)/shard_map/cond/branch_1_fun/all_to_all | solution.py:381
  80.5 1.9 %finish.1 = (bf16[16,128]{1,0:T(8,128)(2,1)}, bf16[32,256,128]{2,1,0:T(8,128)(2,1)}) custom-call(bf16[32,288,128]{2,1,0:T(8,128)(2,1)S(1)} %all-to-all-done.3.arrived_ref, f32[3,16,128]{2,1,0:T(8,128)} %copy-done), custom_call_target="tpu_custom_call" | custom-call | tf_op jit(solution)/shard_map/cond/branch_1_fun/finish/pallas_call | solution.py:350
  (5 shorter events, 0.0 us)
Async XLA Ops:
  0.6 7.9 %collective-permute-start = (bf16[40,2,64,128]{3,2,1,0:T(8,128)(2,1)}, bf16[40,2,64,128]{3,2,1,0:T(8,128)(2,1)S(1)}, u32[]{:S(2)}, u32[]{:S(2)}) collective-permute-start(bf16[40,2,64,128]{3,2,1,0:T(8,128)(2,1)} %bitcast.30), channel_id=1, source_target_pairs={{0,1},{1,0},{2,3},{3,2},{4,5},{5,4},{6,7},{7,6},{8,9},{9,8},{10,11... | collective-permute-start | bytes 3932168 | tf_op jit(solution)/shard_map/ppermute | solution.py:376
  2.6 6.0 %collective-permute-start.1 = (bf16[32,2,64,128]{3,2,1,0:T(8,128)(2,1)}, bf16[32,2,64,128]{3,2,1,0:T(8,128)(2,1)}, u32[]{:S(2)}, u32[]{:S(2)}) collective-permute-start(bf16[32,2,64,128]{3,2,1,0:T(8,128)(2,1)} %bitcast.23), channel_id=1, source_target_pairs={{0,1},{1,0},{2,3},{3,2},{4,5},{5,4},{6,7},{7,6},{8,9},{9,8},{10,11... | collective-permute-start | bytes 3145736 | tf_op jit(solution)/shard_map/ppermute | solution.py:377
  8.6 24.8 %all-to-all-start.2 = ((bf16[32,16,128]{2,1,0:T(8,128)(2,1)}), bf16[32,16,128]{2,1,0:T(8,128)(2,1)S(1)}, u32[]{:S(2)}, u32[]{:S(2)}) async-start(bf16[32,16,128]{2,1,0:T(8,128)(2,1)} %get-tuple-element.52), calls=%async_computation.2 | async-start | bytes 262144 | tf_op jit(solution)/shard_map/cond/branch_1_fun/all_to_all | solution.py:381
  37.3 5.5 %copy-start.2 = (bf16[1,4,2,8,128]{4,3,2,1,0:T(8,128)(2,1)S(1)}, bf16[1,4,2,8,128]{4,3,2,1,0:T(8,128)(2,1)}, u32[]{:S(2)}) copy-start(bf16[1,4,2,8,128]{4,3,2,1,0:T(8,128)(2,1)} %get-tuple-element.130) | copy-start | bytes 49156 | tf_op jit(solution)/shard_map/cond
  37.3 5.5 %copy-start.6 = (s32[32]{0:T(128)S(1)}, s32[32]{0:T(128)}, u32[]{:S(2)}) copy-start(s32[32]{0:T(128)} %get-tuple-element.56) | copy-start | bytes 388 | tf_op jit(solution)/shard_map/cond
  37.3 6.8 %copy-start.4 = (bf16[16,128]{1,0:T(8,128)(2,1)S(1)}, bf16[16,128]{1,0:T(8,128)(2,1)}, u32[]{:S(2)}) copy-start(bf16[16,128]{1,0:T(8,128)(2,1)} %get-tuple-element.57.query_ref) | copy-start | bytes 12292 | tf_op jit(solution)/shard_map/cond
  37.3 43.2 %all-to-all-start.3 = ((bf16[32,288,128]{2,1,0:T(8,128)(2,1)}), bf16[32,288,128]{2,1,0:T(8,128)(2,1)S(1)}, u32[]{:S(2)}, u32[]{:S(2)}) async-start(bf16[32,288,128]{2,1,0:T(8,128)(2,1)} %resident.1), calls=%async_computation.3 | async-start | bytes 4718592 | tf_op jit(solution)/shard_map/cond/branch_1_fun/all_to_all | solution.py:381
  46.4 0.6 copy-start
